TPU v7x, 512 devices: a whole 4x8x8 slice. The times are simulated.
512 devices in a mesh: gx: 32 (over y, x_lo, core), gy: 16 (over z, x_hi).
Axes of the slice: x: 4 (x_hi: 2, x_lo: 2; x = x_hi * 2 + x_lo), y: 8, z: 8, core: 2. Of those that a mesh axis runs over, the one named last changes fastest.
Arguments:
- noisy: float32 [256, 128, 128], P('gx', 'gy'), may hold values from -6 to 6
- weights: float32 [2, 256, 128, 128], P(None, 'gx', 'gy'), may hold values from 0.1 to 1
- filter_in: bfloat16 [2, 64, 27], replicated, may hold values from -1.25 to 1.25
- bias: float32 [2, 64], replicated, may hold values from -3 to 3
- filter_out: bfloat16 [2, 27, 64], replicated, may hold values from -0.75 to 0.75
- upstream: float32 [256, 128, 128], P('gx', 'gy'), may hold values from -6 to 6
Outputs:
- grad_input: float32 [256, 128, 128], P('gx', 'gy')
- grad_w1: float32 [2, 64, 27], replicated
- grad_w2: float32 [2, 27, 64], replicated
- grad_bias: float32 [2, 64], replicated
All inputs are finite; a program needn't handle non-finite values.
Results may differ from a plain program's by a relative error of at most 0.0062.
Values may be sent and summed in bfloat16 or wider, within the bound.
A program may use at most 64 MiB of HBM per device.

v0:
```python
import math

import jax
import jax.numpy as jnp
from jax import lax
from jax.sharding import PartitionSpec as P

TAU = 0.15
LAMB = 1.0


def shifted_2(value, axis, steps):
    count = lax.axis_size(axis)
    leading, last = (max(0, -steps), min(count, count - steps))
    return lax.ppermute(value, axis, [(source, source + steps) for source in range(leading, last)])


def padded_2(array, sides, width):
    for axis, dim in sides:
        size, length = (lax.axis_size(axis), array.shape[dim])
        up = [(i, (i + 1) % size) for i in range(size - 1)]
        down = [(j, i) for i, j in up]
        last = lax.slice_in_dim(array, length - width, length, axis=dim)
        leading = lax.slice_in_dim(array, 0, width, axis=dim)
        before = lax.ppermute(last, axis, up)
        after = lax.ppermute(leading, axis, down)
        array = jnp.concatenate([before, array, after], axis=dim)
    return array


def padding_depth_extent(field):
    widths = [(0, 0)] * (field.ndim - 1) + [(1, 1)]
    return jnp.pad(field, widths)


def stack_offsets(padded, sign):
    n0 = padded.shape[-3] - 2
    n1 = padded.shape[-2] - 2
    n2 = padded.shape[-1] - 2
    parts = []
    for dx in (-1, 0, 1):
        for dy in (-1, 0, 1):
            for dz in (-1, 0, 1):
                a0 = 1 + sign * dx
                a1 = 1 + sign * dy
                a2 = 1 + sign * dz
                parts.append(padded[..., a0 : a0 + n0, a1 : a1 + n1, a2 : a2 + n2])
    return jnp.stack(parts, axis=-4)


def spread_total_sum(padded, sign):
    n0 = padded.shape[-3] - 2
    n1 = padded.shape[-2] - 2
    n2 = padded.shape[-1] - 2
    total = jnp.zeros((n0, n1, n2), jnp.float32)
    index = 0
    for dx in (-1, 0, 1):
        for dy in (-1, 0, 1):
            for dz in (-1, 0, 1):
                a0 = 1 + sign * dx
                a1 = 1 + sign * dy
                a2 = 1 + sign * dz
                total = total + padded[index, a0 : a0 + n0, a1 : a1 + n1, a2 : a2 + n2]
                index += 1
    return total


def stencil_kernel(value_padded, weight_padded):
    value_vertical = padding_depth_extent(value_padded)
    wz = padding_depth_extent(weight_padded)
    flux_x = wz[:-1, 1:-1, 1:-1] * (
        value_vertical[1:, 1:-1, 1:-1] - value_vertical[:-1, 1:-1, 1:-1]
    )
    flux_y = wz[1:-1, :-1, 1:-1] * (
        value_vertical[1:-1, 1:, 1:-1] - value_vertical[1:-1, :-1, 1:-1]
    )
    flux_z = wz[1:-1, 1:-1, :-1] * (
        value_vertical[1:-1, 1:-1, 1:] - value_vertical[1:-1, 1:-1, :-1]
    )
    return (
        flux_x[:-1]
        - flux_x[1:]
        + (flux_y[:, :-1] - flux_y[:, 1:])
        + (flux_z[:, :, :-1] - flux_z[:, :, 1:])
    )


def silu_slope(pre):
    sig = jax.nn.sigmoid(pre)
    return sig * (1.0 + pre * (1.0 - sig))


def features(piece, first, shift, inside):
    lifted = padding_depth_extent(piece.astype(jnp.bfloat16))
    patches = stack_offsets(lifted, 1)
    pre = jnp.einsum("cj,jxyz->cxyz", first, patches, preferred_element_type=jnp.float32)
    pre = pre + shift[:, None, None, None]
    feats = (jax.nn.silu(pre) * inside).astype(jnp.bfloat16)
    return (feats, lifted, pre)


def body(noisy, weights, filter_in, bias, filter_out, upstream):
    tile_x, tile_y, depth = noisy.shape
    layers = weights.shape[0]
    span_x = tile_x * lax.axis_size("gx")
    span_y = tile_y * lax.axis_size("gy")
    xs = lax.axis_index("gx") * tile_x - 1 + jnp.arange(tile_x + 2, dtype=jnp.int32)
    ys = lax.axis_index("gy") * tile_y - 1 + jnp.arange(tile_y + 2, dtype=jnp.int32)
    crossline_mask_rows = ((xs >= 0) & (xs < span_x)).astype(jnp.float32)
    inline_mask_rows = ((ys >= 0) & (ys < span_y)).astype(jnp.float32)
    inside = crossline_mask_rows[:, None, None] * inline_mask_rows[None, :, None]
    lower_x = shifted_2(weights[:, tile_x - 1 :, :, :], "gx", 1)
    lower_y = shifted_2(weights[:, :, tile_y - 1 :, :], "gy", 1)
    weight_pad = jnp.pad(weights, ((0, 0), (1, 1), (1, 1), (0, 0)))
    weight_pad = weight_pad.at[:, 0:1, 1 : tile_y + 1, :].set(lower_x)
    weight_pad = weight_pad.at[:, 1 : tile_x + 1, 0:1, :].set(lower_y)
    field = noisy
    saved_rims = []
    for k in range(layers):
        rims = padded_2(field, (("gx", 0), ("gy", 1)), 2)
        feats, lifted, _ = features(rims, filter_in[k], bias[k], inside)
        mixed = jnp.einsum(
            "jc,cxyz->jxyz", filter_out[k], feats, preferred_element_type=jnp.float32
        )
        learned = spread_total_sum(padding_depth_extent(mixed), 1)
        smooth = stencil_kernel(rims[1:-1, 1:-1], weight_pad[k])
        field = field - TAU * (field - noisy + LAMB * smooth + learned)
        saved_rims.append(rims)
    cot = upstream
    data_grad = jnp.zeros_like(upstream)
    list_in = [None] * layers
    list_out = [None] * layers
    list_bias = [None] * layers
    for k in reversed(range(layers)):
        rims = saved_rims[k]
        feats, lifted, pre = features(rims, filter_in[k], bias[k], inside)
        patch_tile = stack_offsets(lifted[1:-1, 1:-1], 1)
        near = padded_2(cot, (("gx", 0), ("gy", 1)), 1)
        scaled = padding_depth_extent((-TAU * near).astype(jnp.bfloat16))
        shifted = stack_offsets(scaled, -1)
        feat_tile = feats[:, 1:-1, 1:-1]
        dfeat = jnp.einsum(
            "jc,jxyz->cxyz", filter_out[k], shifted, preferred_element_type=jnp.float32
        )
        dfeat = dfeat * silu_slope(pre[:, 1:-1, 1:-1])
        dfeat_b = dfeat.astype(jnp.bfloat16)
        g_out = jnp.einsum("jxyz,cxyz->jc", shifted, feat_tile, preferred_element_type=jnp.float32)
        g_bias = jnp.sum(dfeat, axis=(1, 2, 3))
        g_in = jnp.einsum("cxyz,jxyz->cj", dfeat_b, patch_tile, preferred_element_type=jnp.float32)
        dfeat_rims = padded_2(dfeat_b, (("gx", 1), ("gy", 2)), 1)
        back = jnp.einsum(
            "cj,cxyz->jxyz", filter_in[k], dfeat_rims, preferred_element_type=jnp.float32
        )
        through = spread_total_sum(padding_depth_extent(back), -1)
        smooth = stencil_kernel(near, weight_pad[k])
        data_grad = data_grad + TAU * cot
        cot = cot - TAU * (cot + LAMB * smooth) + through
        g_in, g_out, g_bias = lax.psum((g_in, g_out, g_bias), ("gx", "gy"))
        list_in[k] = g_in
        list_out[k] = g_out
        list_bias[k] = g_bias
    stack_in = jnp.stack(list_in)
    stack_out = jnp.stack(list_out)
    stack_bias = jnp.stack(list_bias)
    scale = 1.0 / math.sqrt(span_x * span_y * depth)
    grad_input = cot + data_grad
    return (grad_input, stack_in * scale, stack_out * scale, stack_bias * scale)


def solution(mesh):
    return jax.shard_map(
        body,
        mesh=mesh,
        in_specs=(
            P("gx", "gy", None),
            P(None, "gx", "gy", None),
            P(),
            P(),
            P(),
            P("gx", "gy", None),
        ),
        out_specs=(P("gx", "gy", None), P(), P(), P()),
        check_vma=False,
    )
```

profile of v0, /device:TPU:1, one launch (start us, length us, event | category | flops | bytes accessed | tf_op | source)
XLA Modules:
  0.0 287.9 jit_solution(17226491428687326046)
XLA Ops:
  1.3 8.8 %collective-permute-start.2 = (f32[1,8,128]{2,1,0:T(8,128)S(1)}, f32[1,8,128]{2,1,0:T(8,128)S(1)}, u32[]{:S(2)}, u32[]{:S(2)}) collective-permute-start(f32[1,8,128]{2,1,0:T(8,128)S(1)} %get-tuple-element.370), channel_id=1, source_target_pairs={{16,0},{32,16},{48,32},{64,48},{80,64},{96,80},{112,96},{128,112},... | collective-permute-start | bytes 12296 | tf_op jit(solution)/shard_map/ppermute | solution.py:26
  12.8 2.4 collective-permute-start.6
  15.2 3.2 %collective-permute-start.7 = (f32[2,8,128]{2,1,0:T(8,128)S(1)}, f32[2,8,128]{2,1,0:T(8,128)S(1)}, u32[]{:S(2)}, u32[]{:S(2)}) collective-permute-start(f32[2,8,128]{2,1,0:T(8,128)S(1)} %get-tuple-element.369), channel_id=1, source_target_pairs={{0,16},{16,32},{32,48},{48,64},{64,80},{80,96},{96,112},{112,128},... | collective-permute-start | bytes 24584 | tf_op jit(solution)/shard_map/ppermute | solution.py:25
  29.1 3.7 %collective-permute-start.5 = (f32[10,1,128]{2,1,0:T(1,128)S(1)}, f32[10,1,128]{2,1,0:T(1,128)S(1)}, u32[]{:S(2)}, u32[]{:S(2)}) collective-permute-start(f32[10,1,128]{2,1,0:T(1,128)S(1)} %get-tuple-element.364), channel_id=1, source_target_pairs={{0,1},{1,2},{2,3},{3,4},{4,5},{5,6},{6,7},{7,8},{8,9},{9,10},{10,1... | collective-permute-start | bytes 15368 | tf_op jit(solution)/shard_map/ppermute | solution.py:25
  35.0 5.5 %collective-permute-start.9 = (f32[12,2,128]{2,1,0:T(2,128)S(1)}, f32[12,2,128]{2,1,0:T(2,128)S(1)}, u32[]{:S(2)}, u32[]{:S(2)}) collective-permute-start(f32[12,2,128]{2,1,0:T(2,128)S(1)} %get-tuple-element.306), channel_id=1, source_target_pairs={{0,1},{1,2},{2,3},{3,4},{4,5},{5,6},{6,7},{7,8},{8,9},{9,10},{10,1... | collective-permute-start | bytes 36872 | tf_op jit(solution)/shard_map/ppermute | solution.py:25
  49.4 2.4 stack.614
  51.8 3.0 %multiply_convert_fusion = (bf16[64,10,10,128]{3,0,2,1:T(8,128)(2,1)S(1)}, f32[64,10,10,128]{3,0,2,1:T(8,128)}) fusion(f32[10,10]{1,0:T(8,128)S(1)} %broadcast_multiply_fusion, f32[64]{0:T(128)S(1)} %get-tuple-element.404, bf16[27,10,10,128]{3,0,2,1:T(8,128)(2,1)S(1)} %stack.614, bf16[1,64,27]{1,0,2:T(2,128)(2,1)S(1)} %get-tuple-element.402), kind=kOutput, calls=%fused_computation.55 | convolution fusion | flops 49971200 | bytes 5610512 | tf_op jit(solution)/shard_map/cj,jxyz->cxyz/dot_general | solution.py:96
  57.9 5.7 %collective-permute-start.10 = (bf16[2,8,128]{2,1,0:T(8,128)(2,1)S(1)}, bf16[2,8,128]{2,1,0:T(8,128)(2,1)S(1)}, u32[]{:S(2)}, u32[]{:S(2)}) collective-permute-start(bf16[2,8,128]{2,1,0:T(8,128)(2,1)S(1)} %get-tuple-element.397), channel_id=1, source_target_pairs={{0,16},{16,32},{32,48},{48,64},{64,80},{80,96},{96,112},{112,128},... | collective-permute-start | bytes 12296 | tf_op jit(solution)/shard_map/ppermute | solution.py:25
  65.7 2.8 collective-permute-done.11
  68.6 6.4 %collective-permute-start.12 = (bf16[12,2,128]{2,1,0:T(2,128)(2,1)S(1)}, bf16[12,2,128]{2,1,0:T(2,128)(2,1)S(1)}, u32[]{:S(2)}, u32[]{:S(2)}) collective-permute-start(bf16[12,2,128]{2,1,0:T(2,128)(2,1)S(1)} %get-tuple-element.393), channel_id=1, source_target_pairs={{0,1},{1,2},{2,3},{3,4},{4,5},{5,6},{6,7},{7,8},{8,9},{9,10},{10,1... | collective-permute-start | bytes 18440 | tf_op jit(solution)/shard_map/ppermute | solution.py:25
  84.5 4.5 %stack.642 = bf16[27,10,10,128]{3,0,2,1:T(8,128)(2,1)S(1)} concatenate(bf16[1,10,10,128]{3,0,2,1:T(2,128)(2,1)S(1)} %copy.1439, bf16[1,10,10,128]{3,0,2,1:T(2,128)(2,1)S(1)} %copy.1440, bf16[1,10,10,128]{3,0,2,1:T(2,128)(2,1)S(1)} %copy.1441, bf16[1,10,10,128]{3,0,2,1:T(2,128)(2,1)S(1)} %copy.1442, bf16[1,10,10,128]{3,0,2,1:T(2,128)(2,1)S(1)} %copy.1443, ...), dimensions={0} | concatenate | bytes 1382400 | tf_op jit(solution)/shard_map/stack | solution.py:48
  91.3 3.1 %collective-permute-start.14 = (bf16[64,1,8,128]{3,0,2,1:T(8,128)(2,1)S(1)}, bf16[64,1,8,128]{3,0,2,1:T(8,128)(2,1)S(1)}, u32[]{:S(2)}, u32[]{:S(2)}) collective-permute-start(bf16[64,1,8,128]{3,0,2,1:T(8,128)(2,1)S(1)} %get-tuple-element.205), channel_id=1, source_target_pairs={{0,16},{16,32},{32,48},{48,64},{64,80},{80,96},{96,112},{112,128},... | collective-permute-start | bytes 393224 | tf_op jit(solution)/shard_map/ppermute | solution.py:25
  97.9 2.9 %collective-permute-done.15 = bf16[64,1,8,128]{3,0,2,1:T(8,128)(2,1)S(1)} collective-permute-done((bf16[64,1,8,128]{3,0,2,1:T(8,128)(2,1)S(1)}, bf16[64,1,8,128]{3,0,2,1:T(8,128)(2,1)S(1)}, u32[]{:S(2)}, u32[]{:S(2)}) %collective-permute-start.15) | collective-permute-done | bytes 131104 | tf_op jit(solution)/shard_map/ppermute | solution.py:26
  100.8 7.3 %collective-permute-start.16 = (bf16[64,10,1,128]{3,0,2,1:T(8,128)(2,1)S(1)}, bf16[64,10,1,128]{3,0,2,1:T(8,128)(2,1)}, u32[]{:S(2)}, u32[]{:S(2)}) collective-permute-start(bf16[64,10,1,128]{3,0,2,1:T(8,128)(2,1)S(1)} %get-tuple-element.201), channel_id=1, source_target_pairs={{0,1},{1,2},{2,3},{3,4},{4,5},{5,6},{6,7},{7,8},{8,9},{9,10},{10,1... | collective-permute-start | bytes 491528 | tf_op jit(solution)/shard_map/ppermute | solution.py:25
  115.9 3.7 %stack.727 = bf16[27,8,8,128]{3,0,2,1:T(8,128)(2,1)S(1)} concatenate(bf16[1,8,8,128]{3,0,2,1:T(2,128)(2,1)S(1)} %copy.1520, bf16[1,8,8,128]{3,0,2,1:T(2,128)(2,1)S(1)} %copy.1521, bf16[1,8,8,128]{3,0,2,1:T(2,128)(2,1)S(1)} %copy.1522, bf16[1,8,8,128]{3,0,2,1:T(2,128)(2,1)S(1)} %copy.1523, bf16[1,8,8,128]{3,0,2,1:T(2,128)(2,1)S(1)} %copy.1524, bf16[1,8,8,128]{3,0,2,1:T(2,128)(2,1)S(1)} %copy.1525, ...), dimensions={0} | concatenate | bytes 884736 | tf_op jit(solution)/shard_map/stack | solution.py:48
  124.4 2.6 collective-permute-start.18
  129.4 5.9 %collective-permute-start.21 = (f32[10,1,128]{2,1,0:T(1,128)S(1)}, f32[10,1,128]{2,1,0:T(1,128)S(1)}, u32[]{:S(2)}, u32[]{:S(2)}) collective-permute-start(f32[10,1,128]{2,1,0:T(1,128)S(1)} %get-tuple-element.335), channel_id=1, source_target_pairs={{0,1},{1,2},{2,3},{3,4},{4,5},{5,6},{6,7},{7,8},{8,9},{9,10},{10,1... | collective-permute-start | bytes 15368 | tf_op jit(solution)/shard_map/ppermute | solution.py:25
  136.6 4.5 %collective-permute-done.20 = f32[10,1,128]{2,1,0:T(1,128)S(1)} collective-permute-done((f32[10,1,128]{2,1,0:T(1,128)S(1)}, f32[10,1,128]{2,1,0:T(1,128)S(1)}, u32[]{:S(2)}, u32[]{:S(2)}) %collective-permute-start.20) | collective-permute-done | bytes 5152 | tf_op jit(solution)/shard_map/ppermute | solution.py:26
  148.9 3.7 %stack.670 = bf16[27,8,8,128]{3,0,2,1:T(8,128)(2,1)S(1)} concatenate(bf16[1,8,8,128]{3,0,2,1:T(2,128)(2,1)S(1)} %copy.1466, bf16[1,8,8,128]{3,0,2,1:T(2,128)(2,1)S(1)} %copy.1467, bf16[1,8,8,128]{3,0,2,1:T(2,128)(2,1)S(1)} %copy.1468, bf16[1,8,8,128]{3,0,2,1:T(2,128)(2,1)S(1)} %copy.1469, bf16[1,8,8,128]{3,0,2,1:T(2,128)(2,1)S(1)} %copy.1470, bf16[1,8,8,128]{3,0,2,1:T(2,128)(2,1)S(1)} %copy.1471, ...), dimensions={0} | concatenate | bytes 884736 | tf_op jit(solution)/shard_map/stack | solution.py:48
  153.0 2.8 fusion.264
  156.2 2.8 collective-permute-start.22
  161.0 113.7 %all-reduce.13 = (f32[1,64,27]{1,2,0:T(8,128)S(1)}, f32[1,64,27]{1,2,0:T(8,128)S(1)}, f32[1,27,64]{2,1,0:T(8,128)S(1)}, f32[1,27,64]{2,1,0:T(8,128)S(1)}, f32[1,64]{1,0:T(1,128)S(1)}, /*index=5*/f32[1,64]{1,0:T(1,128)S(1)}) all-reduce(f32[1,64,27]{1,2,0:T(8,128)S(1)} %convolution_bitcast_fusion.3, ...), channel_id=1, replica_groups=mesh['gx'=32,'gy'=16] {'gx','gy'}, use_global_device_ids=true, to_apply=%region_1.2 | all-reduce | flops 7040 | bytes 56320 | tf_op jit(solution)/shard_map/psum | solution.py:158
  274.8 2.5 collective-permute-start.24
  280.5 4.9 %collective-permute-done.25 = bf16[64,10,1,128]{3,0,2,1:T(8,128)(2,1)S(1)} collective-permute-done((bf16[64,10,1,128]{3,0,2,1:T(8,128)(2,1)S(1)}, bf16[64,10,1,128]{3,0,2,1:T(8,128)(2,1)S(1)}, u32[]{:S(2)}, u32[]{:S(2)}) %collective-permute-start.25) | collective-permute-done | bytes 163872 | tf_op jit(solution)/shard_map/ppermute | solution.py:26
  (312 shorter events, 76.5 us)
Async XLA Ops:
  1.3 27.7 %collective-permute-start.2 = (f32[1,8,128]{2,1,0:T(8,128)S(1)}, f32[1,8,128]{2,1,0:T(8,128)S(1)}, u32[]{:S(2)}, u32[]{:S(2)}) collective-permute-start(f32[1,8,128]{2,1,0:T(8,128)S(1)} %get-tuple-element.370), channel_id=1, source_target_pairs={{16,0},{32,16},{48,32},{64,48},{80,64},{96,80},{112,96},{128,112},... | collective-permute-start | bytes 12296 | tf_op jit(solution)/shard_map/ppermute | solution.py:26
  10.1 16.9 %collective-permute-start.3 = (f32[1,8,128]{2,1,0:T(8,128)S(1)}, f32[1,8,128]{2,1,0:T(8,128)S(1)}, u32[]{:S(2)}, u32[]{:S(2)}) collective-permute-start(f32[1,8,128]{2,1,0:T(8,128)S(1)} %get-tuple-element.371), channel_id=1, source_target_pairs={{0,16},{16,32},{32,48},{48,64},{64,80},{80,96},{96,112},{112,128},... | collective-permute-start | bytes 12296 | tf_op jit(solution)/shard_map/ppermute | solution.py:25
  12.8 22.2 %collective-permute-start.6 = (f32[2,8,128]{2,1,0:T(8,128)S(1)}, f32[2,8,128]{2,1,0:T(8,128)S(1)}, u32[]{:S(2)}, u32[]{:S(2)}) collective-permute-start(f32[2,8,128]{2,1,0:T(8,128)S(1)} %get-tuple-element.368), channel_id=1, source_target_pairs={{16,0},{32,16},{48,32},{64,48},{80,64},{96,80},{112,96},{128,112},... | collective-permute-start | bytes 24584 | tf_op jit(solution)/shard_map/ppermute | solution.py:26
  15.2 17.7 %collective-permute-start.7 = (f32[2,8,128]{2,1,0:T(8,128)S(1)}, f32[2,8,128]{2,1,0:T(8,128)S(1)}, u32[]{:S(2)}, u32[]{:S(2)}) collective-permute-start(f32[2,8,128]{2,1,0:T(8,128)S(1)} %get-tuple-element.369), channel_id=1, source_target_pairs={{0,16},{16,32},{32,48},{48,64},{64,80},{80,96},{96,112},{112,128},... | collective-permute-start | bytes 24584 | tf_op jit(solution)/shard_map/ppermute | solution.py:25
  19.0 21.4 %collective-permute-start = (f32[2,1,8,128]{3,2,1,0:T(8,128)S(1)}, f32[2,1,8,128]{3,2,1,0:T(8,128)S(1)}, u32[]{:S(2)}, u32[]{:S(2)}) collective-permute-start(f32[2,1,8,128]{3,2,1,0:T(8,128)S(1)} %slice.1260), channel_id=1, source_target_pairs={{0,16},{16,32},{32,48},{48,64},{64,80},{80,96},{96,112},{112,128},... | collective-permute-start | bytes 24584 | tf_op jit(solution)/shard_map/ppermute | solution.py:15
  27.0 16.2 %collective-permute-start.1 = (f32[2,8,1,128]{3,2,1,0:T(1,128)S(1)}, f32[2,8,1,128]{3,2,1,0:T(1,128)S(1)}, u32[]{:S(2)}, u32[]{:S(2)}) collective-permute-start(f32[2,8,1,128]{3,2,1,0:T(1,128)S(1)} %slice.1263), channel_id=1, source_target_pairs={{0,1},{1,2},{2,3},{3,4},{4,5},{5,6},{6,7},{7,8},{8,9},{9,10},{10,1... | collective-permute-start | bytes 24584 | tf_op jit(solution)/shard_map/ppermute | solution.py:15
  29.1 15.9 %collective-permute-start.5 = (f32[10,1,128]{2,1,0:T(1,128)S(1)}, f32[10,1,128]{2,1,0:T(1,128)S(1)}, u32[]{:S(2)}, u32[]{:S(2)}) collective-permute-start(f32[10,1,128]{2,1,0:T(1,128)S(1)} %get-tuple-element.364), channel_id=1, source_target_pairs={{0,1},{1,2},{2,3},{3,4},{4,5},{5,6},{6,7},{7,8},{8,9},{9,10},{10,1... | collective-permute-start | bytes 15368 | tf_op jit(solution)/shard_map/ppermute | solution.py:25
  32.9 12.1 %collective-permute-start.4 = (f32[10,1,128]{2,1,0:T(1,128)S(1)}, f32[10,1,128]{2,1,0:T(1,128)S(1)}, u32[]{:S(2)}, u32[]{:S(2)}) collective-permute-start(f32[10,1,128]{2,1,0:T(1,128)S(1)} %get-tuple-element.365), channel_id=1, source_target_pairs={{1,0},{2,1},{3,2},{4,3},{5,4},{6,5},{7,6},{8,7},{9,8},{10,9},{11,1... | collective-permute-start | bytes 15368 | tf_op jit(solution)/shard_map/ppermute | solution.py:26
  35.0 12.6 %collective-permute-start.9 = (f32[12,2,128]{2,1,0:T(2,128)S(1)}, f32[12,2,128]{2,1,0:T(2,128)S(1)}, u32[]{:S(2)}, u32[]{:S(2)}) collective-permute-start(f32[12,2,128]{2,1,0:T(2,128)S(1)} %get-tuple-element.306), channel_id=1, source_target_pairs={{0,1},{1,2},{2,3},{3,4},{4,5},{5,6},{6,7},{7,8},{8,9},{9,10},{10,1... | collective-permute-start | bytes 36872 | tf_op jit(solution)/shard_map/ppermute | solution.py:25
  40.5 7.1 %collective-permute-start.8 = (f32[12,2,128]{2,1,0:T(2,128)S(1)}, f32[12,2,128]{2,1,0:T(2,128)S(1)}, u32[]{:S(2)}, u32[]{:S(2)}) collective-permute-start(f32[12,2,128]{2,1,0:T(2,128)S(1)} %get-tuple-element.307), channel_id=1, source_target_pairs={{1,0},{2,1},{3,2},{4,3},{5,4},{6,5},{7,6},{8,7},{9,8},{10,9},{11,1... | collective-permute-start | bytes 36872 | tf_op jit(solution)/shard_map/ppermute | solution.py:26
  57.9 7.8 %collective-permute-start.10 = (bf16[2,8,128]{2,1,0:T(8,128)(2,1)S(1)}, bf16[2,8,128]{2,1,0:T(8,128)(2,1)S(1)}, u32[]{:S(2)}, u32[]{:S(2)}) collective-permute-start(bf16[2,8,128]{2,1,0:T(8,128)(2,1)S(1)} %get-tuple-element.397), channel_id=1, source_target_pairs={{0,16},{16,32},{32,48},{48,64},{64,80},{80,96},{96,112},{112,128},... | collective-permute-start | bytes 12296 | tf_op jit(solution)/shard_map/ppermute | solution.py:25
  68.6 10.2 %collective-permute-start.12 = (bf16[12,2,128]{2,1,0:T(2,128)(2,1)S(1)}, bf16[12,2,128]{2,1,0:T(2,128)(2,1)S(1)}, u32[]{:S(2)}, u32[]{:S(2)}) collective-permute-start(bf16[12,2,128]{2,1,0:T(2,128)(2,1)S(1)} %get-tuple-element.393), channel_id=1, source_target_pairs={{0,1},{1,2},{2,3},{3,4},{4,5},{5,6},{6,7},{7,8},{8,9},{9,10},{10,1... | collective-permute-start | bytes 18440 | tf_op jit(solution)/shard_map/ppermute | solution.py:25
  74.9 6.0 %collective-permute-start.13 = (bf16[12,2,128]{2,1,0:T(2,128)(2,1)S(1)}, bf16[12,2,128]{2,1,0:T(2,128)(2,1)S(1)}, u32[]{:S(2)}, u32[]{:S(2)}) collective-permute-start(bf16[12,2,128]{2,1,0:T(2,128)(2,1)S(1)} %get-tuple-element.394), channel_id=1, source_target_pairs={{1,0},{2,1},{3,2},{4,3},{5,4},{6,5},{7,6},{8,7},{9,8},{10,9},{11,1... | collective-permute-start | bytes 18440 | tf_op jit(solution)/shard_map/ppermute | solution.py:26
  91.3 6.5 %collective-permute-start.14 = (bf16[64,1,8,128]{3,0,2,1:T(8,128)(2,1)S(1)}, bf16[64,1,8,128]{3,0,2,1:T(8,128)(2,1)S(1)}, u32[]{:S(2)}, u32[]{:S(2)}) collective-permute-start(bf16[64,1,8,128]{3,0,2,1:T(8,128)(2,1)S(1)} %get-tuple-element.205), channel_id=1, source_target_pairs={{0,16},{16,32},{32,48},{48,64},{64,80},{80,96},{96,112},{112,128},... | collective-permute-start | bytes 393224 | tf_op jit(solution)/shard_map/ppermute | solution.py:25
  94.5 6.3 %collective-permute-start.15 = (bf16[64,1,8,128]{3,0,2,1:T(8,128)(2,1)S(1)}, bf16[64,1,8,128]{3,0,2,1:T(8,128)(2,1)S(1)}, u32[]{:S(2)}, u32[]{:S(2)}) collective-permute-start(bf16[64,1,8,128]{3,0,2,1:T(8,128)(2,1)S(1)} %get-tuple-element.206), channel_id=1, source_target_pairs={{16,0},{32,16},{48,32},{64,48},{80,64},{96,80},{112,96},{128,112},... | collective-permute-start | bytes 393224 | tf_op jit(solution)/shard_map/ppermute | solution.py:26
  100.8 18.8 %collective-permute-start.16 = (bf16[64,10,1,128]{3,0,2,1:T(8,128)(2,1)S(1)}, bf16[64,10,1,128]{3,0,2,1:T(8,128)(2,1)}, u32[]{:S(2)}, u32[]{:S(2)}) collective-permute-start(bf16[64,10,1,128]{3,0,2,1:T(8,128)(2,1)S(1)} %get-tuple-element.201), channel_id=1, source_target_pairs={{0,1},{1,2},{2,3},{3,4},{4,5},{5,6},{6,7},{7,8},{8,9},{9,10},{10,1... | collective-permute-start | bytes 491528 | tf_op jit(solution)/shard_map/ppermute | solution.py:25
  108.1 11.5 %collective-permute-start.17 = (bf16[64,10,1,128]{3,0,2,1:T(8,128)(2,1)S(1)}, bf16[64,10,1,128]{3,0,2,1:T(8,128)(2,1)}, u32[]{:S(2)}, u32[]{:S(2)}) collective-permute-start(bf16[64,10,1,128]{3,0,2,1:T(8,128)(2,1)S(1)} %get-tuple-element.202), channel_id=1, source_target_pairs={{1,0},{2,1},{3,2},{4,3},{5,4},{6,5},{7,6},{8,7},{9,8},{10,9},{11,1... | collective-permute-start | bytes 491528 | tf_op jit(solution)/shard_map/ppermute | solution.py:26
  122.5 5.0 %collective-permute-start.19 = (f32[1,8,128]{2,1,0:T(8,128)S(1)}, f32[1,8,128]{2,1,0:T(8,128)S(1)}, u32[]{:S(2)}, u32[]{:S(2)}) collective-permute-start(f32[1,8,128]{2,1,0:T(8,128)S(1)} %get-tuple-element.366), channel_id=1, source_target_pairs={{0,16},{16,32},{32,48},{48,64},{64,80},{80,96},{96,112},{112,128},... | collective-permute-start | bytes 12296 | tf_op jit(solution)/shard_map/ppermute | solution.py:25
  129.4 7.2 %collective-permute-start.21 = (f32[10,1,128]{2,1,0:T(1,128)S(1)}, f32[10,1,128]{2,1,0:T(1,128)S(1)}, u32[]{:S(2)}, u32[]{:S(2)}) collective-permute-start(f32[10,1,128]{2,1,0:T(1,128)S(1)} %get-tuple-element.335), channel_id=1, source_target_pairs={{0,1},{1,2},{2,3},{3,4},{4,5},{5,6},{6,7},{7,8},{8,9},{9,10},{10,1... | collective-permute-start | bytes 15368 | tf_op jit(solution)/shard_map/ppermute | solution.py:25
  135.3 5.9 %collective-permute-start.20 = (f32[10,1,128]{2,1,0:T(1,128)S(1)}, f32[10,1,128]{2,1,0:T(1,128)S(1)}, u32[]{:S(2)}, u32[]{:S(2)}) collective-permute-start(f32[10,1,128]{2,1,0:T(1,128)S(1)} %get-tuple-element.336), channel_id=1, source_target_pairs={{1,0},{2,1},{3,2},{4,3},{5,4},{6,5},{7,6},{8,7},{9,8},{10,9},{11,1... | collective-permute-start | bytes 15368 | tf_op jit(solution)/shard_map/ppermute | solution.py:26
  156.2 118.5 %collective-permute-start.22 = (bf16[64,1,8,128]{3,0,2,1:T(8,128)(2,1)S(1)}, bf16[64,1,8,128]{3,0,2,1:T(8,128)(2,1)S(1)}, u32[]{:S(2)}, u32[]{:S(2)}) collective-permute-start(bf16[64,1,8,128]{3,0,2,1:T(8,128)(2,1)S(1)} %get-tuple-element.203), channel_id=1, source_target_pairs={{0,16},{16,32},{32,48},{48,64},{64,80},{80,96},{96,112},{112,128},... | collective-permute-start | bytes 393224 | tf_op jit(solution)/shard_map/ppermute | solution.py:25
  159.0 115.7 %collective-permute-start.23 = (bf16[64,1,8,128]{3,0,2,1:T(8,128)(2,1)S(1)}, bf16[64,1,8,128]{3,0,2,1:T(8,128)(2,1)S(1)}, u32[]{:S(2)}, u32[]{:S(2)}) collective-permute-start(bf16[64,1,8,128]{3,0,2,1:T(8,128)(2,1)S(1)} %get-tuple-element.204), channel_id=1, source_target_pairs={{16,0},{32,16},{48,32},{64,48},{80,64},{96,80},{112,96},{128,112},... | collective-permute-start | bytes 393224 | tf_op jit(solution)/shard_map/ppermute | solution.py:26
  274.8 5.7 %collective-permute-start.24 = (bf16[64,10,1,128]{3,0,2,1:T(8,128)(2,1)S(1)}, bf16[64,10,1,128]{3,0,2,1:T(8,128)(2,1)S(1)}, u32[]{:S(2)}, u32[]{:S(2)}) collective-permute-start(bf16[64,10,1,128]{3,0,2,1:T(8,128)(2,1)S(1)} %get-tuple-element.199), channel_id=1, source_target_pairs={{0,1},{1,2},{2,3},{3,4},{4,5},{5,6},{6,7},{7,8},{8,9},{9,10},{10,1... | collective-permute-start | bytes 491528 | tf_op jit(solution)/shard_map/ppermute | solution.py:25
  277.3 8.1 %collective-permute-start.25 = (bf16[64,10,1,128]{3,0,2,1:T(8,128)(2,1)S(1)}, bf16[64,10,1,128]{3,0,2,1:T(8,128)(2,1)S(1)}, u32[]{:S(2)}, u32[]{:S(2)}) collective-permute-start(bf16[64,10,1,128]{3,0,2,1:T(8,128)(2,1)S(1)} %get-tuple-element.200), channel_id=1, source_target_pairs={{1,0},{2,1},{3,2},{4,3},{5,4},{6,5},{7,6},{8,7},{9,8},{10,9},{11,1... | collective-permute-start | bytes 491528 | tf_op jit(solution)/shard_map/ppermute | solution.py:26
  (19 other events, 573.2 us)
where the time goes:
time: 292 us; the launch traced here: 288 us
  blocking collectives  114 us (39%)
  starting transfers between devices  80.5 us (28%)
  local copies, waits for them, and re-layouts  51.2 us (18%)
  waiting for transfers between devices  19.2 us (7%)
  matrix products  12.8 us (4%)
  other arithmetic  7.75 us (3%)
    psum x1, blocking collectives, body(): g_in, g_out, g_bias = lax.psum((g_in, g_out, g_bias), ('gx', 'gy'))  114 us
    ppermute x12, starting transfers between devices, padded_2(): before = lax.ppermute(last, axis, up)  49.9 us
    another operation x179, local copies, waits for them, and re-layouts, stack_offsets(): return jnp.stack(parts, axis=-4)  36.9 us
    ppermute x12, starting transfers between devices, padded_2(): after = lax.ppermute(leading, axis, down)  27.5 us
    ppermute x12, waiting for transfers between devices, padded_2(): after = lax.ppermute(leading, axis, down)  19.1 us
  transfers between devices with their start and end apart: 26, of which 6 were waited for; matrix products, arithmetic and copies ran while one was open for 11% of the time, Pallas kernels for 0%

commit v1 on v0

v1 whole, which is shorter than its diff:
```python
import functools

import jax
import jax.numpy as jnp
from jax import lax
from jax.experimental import pallas as pl
from jax.experimental.pallas import tpu as pltpu
from jax.sharding import PartitionSpec as P

TAU = 0.15
F32 = jnp.float32
BF16 = jnp.bfloat16
MESH = pl.DeviceIdType.MESH
CH = 64
ROWS = 24
XOFF = 5
LAYERS_X = 18
SLAB = 80
DEPTH = 3 * SLAB


def iota(shape, axis):
    return lax.broadcasted_iota(jnp.int32, shape, axis)


def move_z(v, step):
    lane = iota(v.shape, 1)
    if step == 1:
        return jnp.where(lane == 127, 0.0, pltpu.roll(v, 127, 1))
    return jnp.where(lane == 0, 0.0, pltpu.roll(v, 1, 1))


def move_y(v, step):
    return pltpu.roll(v, (-step) % v.shape[0], 0)


def slab_of(v):
    ones = jnp.ones((SLAB - 3 * ROWS, 128), F32)
    return jnp.concatenate([move_z(v, -1), v, move_z(v, 1), ones], axis=0).astype(BF16)


def flux_x(v, w, i):
    return w[i] * (v[i + 1] - v[i])


def smooth_at(v, w, i):
    here, factor = v[i], w[i]
    fy = factor * (move_y(here, 1) - here)
    fz = factor * (move_z(here, 1) - here)
    return (
        flux_x(v, w, i - 1) - flux_x(v, w, i) + (move_y(fy, -1) - fy) + (move_z(fz, -1) - fz)
    )


def split_column(shape, axis):
    k = iota(shape, axis)
    sx = (k >= SLAB).astype(jnp.int32) + (k >= 2 * SLAB).astype(jnp.int32)
    rest = k - SLAB * sx
    sz = (rest >= ROWS).astype(jnp.int32) + (rest >= 2 * ROWS).astype(jnp.int32)
    row = rest - ROWS * sz
    good = (rest < 3 * ROWS) & (k < DEPTH)
    return sx, sz, row, good, rest


def split_rows(shape, axis):
    m = iota(shape, axis)
    s = sum((m >= ROWS * n).astype(jnp.int32) for n in range(1, 9))
    row = m - ROWS * s
    sx = (s >= 3).astype(jnp.int32) + (s >= 6).astype(jnp.int32)
    return sx, s - 3 * sx, row


def one_hot(hit):
    return jnp.where(hit, 1.0, 0.0).astype(BF16)


def dot(a, b):
    return jnp.dot(a, b, preferred_element_type=F32)


def dot_nt(a, b):
    return lax.dot_general(a, b, (((1,), (1,)), ((), ())), preferred_element_type=F32)


def thirds(v):
    high = v.astype(BF16)
    rest = v - high.astype(F32)
    mid = rest.astype(BF16)
    low = (rest - mid.astype(F32)).astype(BF16)
    return high, mid, low


def fill_patch(out, weight, bias_col, ys):
    shape = (32, DEPTH)
    sx, sz, row, good, _ = split_column(shape, 1)
    base = 9 * sx + sz
    j = iota(shape, 0)
    k = iota((CH, DEPTH), 1)
    extra = jnp.zeros((CH, DEPTH), F32)
    for n, part in enumerate(thirds(bias_col)):
        extra = extra + jnp.where(k == SLAB + 3 * ROWS + n, part.astype(F32), 0.0)
    for n, y in enumerate(ys):
        step = row - (y + 7)
        hit = good & (step >= 0) & (step <= 2) & (j == base + 3 * step)
        block = (dot(weight, one_hot(hit)) + extra) * 0.5
        out[n * CH : (n + 1) * CH, :] = block.astype(BF16)


def fill_spread(out, weight_t, ys):
    shape = (32, DEPTH)
    sx, sz, row, good, _ = split_column(shape, 1)
    base = 9 * (2 - sx) + (2 - sz)
    j = iota(shape, 0)
    for n, y in enumerate(ys):
        step = (y + 9) - row
        hit = good & (step >= 0) & (step <= 2) & (j == base + 3 * step)
        out[n * CH : (n + 1) * CH, :] = (dot(weight_t, one_hot(hit)) * 0.5).astype(BF16)


def fill_gather(out, weight, ys, sign, low, high):
    shape = (9 * ROWS, 32)
    sx, sz, row = split_rows(shape, 0)
    base = 9 * sx + sz
    j = iota(shape, 1)
    for n in range(0, len(ys), 2):
        halves = []
        for y in ys[n : n + 2]:
            step = (y + 9) - row if sign > 0 else row - (y + 7)
            hit = (step >= 0) & (step <= 2) & (j == base + 3 * step)
            part = one_hot(hit)
            half = dot(part, weight) if sign > 0 else dot_nt(part, weight)
            if y < 0:
                half = half * low
            elif y > 7:
                half = half * high
            halves.append(half)
        out[:, n * CH : (n + 2) * CH] = jnp.concatenate(halves, axis=1).astype(BF16)


def pair_of(stack, i):
    left = stack[pl.ds(i - 1, 3)].reshape(DEPTH, 128)
    right = stack[pl.ds(i, 3)].reshape(DEPTH, 128)
    return jnp.concatenate([left, right], axis=1)


def gather_sum(store, n, sign):
    total = None
    for sz in range(3):
        part = None
        for sx in range(3):
            at = n + sx if sign > 0 else n + 2 - sx
            lo = (3 * sx + sz) * ROWS
            term = store[at, lo : lo + ROWS, :]
            part = term if part is None else part + term
        if sz != 1:
            part = move_z(part, sign * (sz - 1))
        total = part if total is None else total + part
    return total


def fold_rows(out):
    total = out[0:CH]
    for y in range(1, 8):
        total = total + pltpu.roll(out[y * CH : (y + 1) * CH], 256 - y, 1)
    return total


def pick_columns(layer, first):
    shape = (256, 128)
    sx, sz, row, good, rest = split_column(shape, 0)
    lane = iota(shape, 1)
    if first:
        step = row - 7
        j = 9 * sx + 3 * step + sz
        ok = good & (step >= 0) & (step <= 2)
        hit = ok & (lane == 64 * layer + j)
        spare = (sx == 1) & (rest == 3 * ROWS) & (lane == 64 * layer + 27)
        return one_hot(hit | spare)
    step = 9 - row
    j = 9 * (2 - sx) + 3 * step + (2 - sz)
    ok = good & (step >= 0) & (step <= 2)
    return one_hot(ok & (lane == 64 * layer + 32 + j))


def packed_sums(out, layer, first):
    folded = fold_rows(out)
    pick = pick_columns(layer, first)
    high, mid, low = thirds(folded)
    return dot(high, pick) + dot(mid, pick) + dot(low, pick)


def layers_beside(stack):
    parts = [stack[i - 1 : i + 2].reshape(DEPTH, 128) for i in range(XOFF, XOFF + 8)]
    whole = jnp.concatenate(parts, axis=1)
    return jnp.concatenate([whole, jnp.zeros((256 - DEPTH, 1024), BF16)], axis=0)


def kernel(
    size_x, size_y,
    noisy, weights, filter_in, bias, filter_out, upstream,
    out_grad, out_w1, out_w2, out_b,
    send_x, send_yl, send_yh, got_x, got_y,
    u0, g0, w0, w1, u1, g1,
    su0, ss1, su1, ss0,
    t1a, t1b, t2b, t2a, toa, t3b, t3a,
    pad_in, pad_out,
    qbuf, pbuf, h0, d0, h1, dab1, dab0,
    ring_x, ring_y, ring_c, back_x, back_y, back_c, part,
    pack, red_g, red_y, red_z, tile_y, tile_z, tile_f, final,
    halo_send, halo_recv, ring_send, ring_recv, red_send, red_recv,
):
    gx, gy = lax.axis_index("gx"), lax.axis_index("gy")
    core, xlo, py = lax.rem(gx, 2), lax.rem(gx // 2, 2), gx // 4
    xhi, pz = lax.rem(gy, 2), gy // 2
    ny, nz = size_x // 4, size_y // 2
    me_g = (xhi * 2 + xlo) * 2 + core

    def near(dx, dy):
        return (lax.rem(gx + dx + size_x, size_x), lax.rem(gy + dy + size_y, size_y))

    def in_group(step):
        to = lax.rem(me_g + step, 8)
        c, x = lax.rem(to, 2), to // 2
        return to, (py * 4 + lax.rem(x, 2) * 2 + c, pz * 2 + x // 2)

    def along_y(step):
        return (lax.rem(py + step, ny) * 4 + xlo * 2 + core, gy)

    def along_z(step):
        return (gx, lax.rem(pz + step, nz) * 2 + xhi)

    sides = [(dx, dy) for dx in (-1, 0, 1) for dy in (-1, 0, 1) if (dx, dy) != (0, 0)]
    barrier = pltpu.get_barrier_semaphore()
    peers = [near(*side) for side in sides] + [in_group(s)[1] for s in range(1, 8)]
    peers += [along_y(s) for s in range(1, ny)] + [along_z(s) for s in range(1, nz)]
    for peer in peers:
        pl.semaphore_signal(barrier, inc=1, device_id=peer, device_id_type=MESH)

    mxl = jnp.where(gx > 0, 1.0, 0.0).astype(F32)
    mxh = jnp.where(gx < size_x - 1, 1.0, 0.0).astype(F32)
    myl = jnp.where(gy > 0, 1.0, 0.0).astype(F32)
    myh = jnp.where(gy < size_y - 1, 1.0, 0.0).astype(F32)

    row8 = iota((8, 128), 0)
    for x in range(8):
        u, g, wa, wb = noisy[x], upstream[x], weights[0, x], weights[1, x]
        send_x[x] = jnp.concatenate([u, g, wa, wb], axis=0).astype(BF16)
        top = jnp.where(row8 < 5, pltpu.roll(u, 5, 0), g)
        low = jnp.where(row8 < 4, pltpu.roll(wa, 4, 0), pltpu.roll(wb, 6, 0))
        send_yl[x] = jnp.concatenate([top, low], axis=0).astype(BF16)
        top = jnp.where(row8 < 5, u, pltpu.roll(g, 5, 0))
        low = jnp.where(row8 < 4, wa, pltpu.roll(wb, 4, 0))
        send_yh[x] = jnp.concatenate([top, low], axis=0).astype(BF16)
    pl.semaphore_wait(barrier, len(peers))

    halo = []
    span = {-1: (0, 13), 0: (0, 5), 1: (3, 0)}
    for n, (dx, dy) in enumerate(sides):
        start, land = span[dx]
        if dy == 0:
            src, dst = send_x.at[pl.ds(start, 5)], got_x.at[0 if dx > 0 else 1]
        else:
            count = 8 if dx == 0 else 5
            src = (send_yl if dy > 0 else send_yh).at[pl.ds(start, count)]
            dst = got_y.at[0 if dy > 0 else 1, pl.ds(land, count)]
        copy = pltpu.make_async_remote_copy(
            src_ref=src, dst_ref=dst, send_sem=halo_send.at[n], recv_sem=halo_recv.at[n],
            device_id=near(dx, dy), device_id_type=MESH,
        )
        copy.start()
        halo.append(copy)

    eye = iota((CH, CH), 0) == iota((CH, CH), 1)
    pad_in[...] = jnp.zeros_like(pad_in)
    pad_out[...] = jnp.zeros_like(pad_out)
    cols = []
    for k in range(2):
        pad_in[k, :, 0:27] = filter_in[k].astype(F32)
        pad_out[k, 0:27, :] = filter_out[k].astype(F32)
        spread = jnp.broadcast_to(bias[k : k + 1, :], (CH, CH))
        cols.append(jnp.sum(jnp.where(eye, spread, 0.0), axis=1, keepdims=True))
    win = [pad_in[k, :, 0:32].astype(BF16) for k in range(2)]
    wout = [pad_out[k].astype(BF16) for k in range(2)]
    wout_t = [dot_nt(one_hot(eye), wout[k]).astype(BF16) for k in range(2)]
    fill_patch(t1a, win[0], cols[0], range(-4, 12))
    fill_gather(toa, wout[0], range(-4, 12), 1, myl, myh)
    fill_patch(t1b, win[1], cols[1], range(-2, 10))
    fill_spread(t2b, wout_t[1], range(-2, 10))
    fill_gather(t3b, win[1], range(-2, 10), -1, myl, myh)
    fill_spread(t2a, wout_t[0], range(0, 8))
    fill_gather(t3a, win[0], range(0, 8), -1, myl, myh)

    for copy in halo:
        copy.wait()

    for i in range(LAYERS_X):
        if i < XOFF:
            rows, edge = got_x[0, i].astype(F32) * mxl, mxl
        elif i >= XOFF + 8:
            rows, edge = got_x[1, i - XOFF - 8].astype(F32) * mxh, mxh
        else:
            x, edge = i - XOFF, jnp.float32(1.0)
            rows = jnp.concatenate([noisy[x], upstream[x], weights[0, x], weights[1, x]], axis=0)
        lo = got_y[0, i].astype(F32) * (edge * myl)
        hi = got_y[1, i].astype(F32) * (edge * myh)
        lo_t, lo_b, hi_t, hi_b = lo[0:8], lo[8:16], hi[0:8], hi[8:16]
        u = jnp.concatenate([pltpu.roll(lo_t, 3, 0), rows[0:8], hi_t], axis=0)
        u0[i] = u
        su0[i] = slab_of(u)
        w0[i] = jnp.concatenate([pltpu.roll(lo_b, 4, 0), rows[16:24], hi_b], axis=0)
        if 2 <= i < 16:
            g = jnp.concatenate([lo_t, rows[8:16], pltpu.roll(hi_t, 3, 0)], axis=0)
            g0[i] = g
            ss1[i] = slab_of(-TAU * g)
            w1[i] = jnp.concatenate(
                [pltpu.roll(lo_b, 2, 0), rows[24:32], pltpu.roll(hi_b, 4, 0)], axis=0
            )

    row24 = iota((ROWS, 128), 0)
    inside_y = jnp.where(row24 < 8, myl, jnp.where(row24 < 16, 1.0, myh))

    def x_mask(i):
        return jnp.where(i < XOFF, mxl, jnp.where(i >= XOFF + 8, mxh, 1.0))

    def forward(p, keep):
        i = 1 + 2 * p
        half = dot(t1a[...], pair_of(su0, i))
        t = jnp.tanh(half)
        h = half + half * t
        hb = h.astype(BF16)
        if keep:
            tile = slice(4 * CH, 12 * CH)
            h0[p - 2] = hb[tile]
            d0[p - 2] = (1.0 + t[tile]) + (h[tile] - h[tile] * t[tile])
        q = dot(toa[...], hb)
        qbuf[2 * p] = q[:, 0:128] * x_mask(i)
        qbuf[2 * p + 1] = q[:, 128:256] * x_mask(i + 1)

    @pl.loop(0, 4)
    def _(n):
        forward(jnp.where(n < 2, n, n + 4), False)

    @pl.loop(2, 6)
    def _(p):
        forward(p, True)

    for i in range(2, 16):
        learned = gather_sum(qbuf, i - 2, 1)
        v = u0[i] - TAU * (smooth_at(u0, w0, i) + learned)
        v = v * inside_y
        if i < XOFF:
            v = v * mxl
        elif i >= XOFF + 8:
            v = v * mxh
        su1[i] = slab_of(v)

    def middle(p, keep):
        i = 3 + 2 * p
        half = dot(t1b[...], pair_of(su1, i))
        dh = dot(t2b[...], pair_of(ss1, i))
        t = jnp.tanh(half)
        h = half + half * t
        dab = (dh * ((1.0 + t) + (h - h * t))).astype(BF16)
        if keep:
            tile = slice(2 * CH, 10 * CH)
            h1[p - 1] = h[tile].astype(BF16)
            dab1[p - 1] = dab[tile]
        q = dot(t3b[...], dab)
        pbuf[2 * p] = q[:, 0:128] * x_mask(i)
        pbuf[2 * p + 1] = q[:, 128:256] * x_mask(i + 1)

    @pl.loop(0, 2)
    def _(n):
        middle(n * 5, False)

    @pl.loop(1, 5)
    def _(p):
        middle(p, True)

    for i in range(4, 14):
        g = g0[i]
        v = g - TAU * (g + smooth_at(g0, w1, i)) + gather_sum(pbuf, i - 4, -1)
        v = v * inside_y
        if i < XOFF:
            v = v * mxl
        elif i >= XOFF + 8:
            v = v * mxh
        g1[i] = v
        ss0[i] = slab_of(-TAU * v)

    @pl.loop(0, 4)
    def _(p):
        dh = dot(t2a[...], pair_of(ss0, XOFF + 2 * p))
        dab0[p] = (dh * d0[p]).astype(BF16)

    def beside(store):
        return jnp.concatenate([store[p] for p in range(4)], axis=1)

    sums = packed_sums(dot_nt(beside(h0), layers_beside(ss0)), 0, False)
    sums = sums + packed_sums(dot_nt(beside(dab0), layers_beside(su0)), 0, True)
    sums = sums + packed_sums(dot_nt(beside(h1), layers_beside(ss1)), 1, False)
    sums = sums + packed_sums(dot_nt(beside(dab1), layers_beside(su1)), 1, True)
    for n in range(8):
        pack[n] = sums[8 * n : 8 * n + 8]

    first = []
    for s in range(1, 8):
        to, peer = in_group(s)
        copy = pltpu.make_async_remote_copy(
            src_ref=pack.at[to], dst_ref=red_g.at[me_g],
            send_sem=red_send.at[0, s], recv_sem=red_recv.at[0, s],
            device_id=peer, device_id_type=MESH,
        )
        copy.start()
        first.append(copy)
    red_g[me_g] = pack[me_g]

    pbuf[0] = jnp.zeros_like(pbuf[0])
    pbuf[1] = jnp.zeros_like(pbuf[1])
    pbuf[10] = jnp.zeros_like(pbuf[0])
    pbuf[11] = jnp.zeros_like(pbuf[0])

    @pl.loop(0, 4)
    def _(p):
        q = dot(t3a[...], dab0[p])
        pbuf[2 * p + 2] = q[:, 0:128]
        pbuf[2 * p + 3] = q[:, 128:256]

    for n in range(10):
        part[n] = gather_sum(pbuf, n, -1)
    ring_x[0] = part[0, 8:16, :]
    ring_x[1] = part[9, 8:16, :]
    for side, row in ((0, 7), (1, 16)):
        ring_y[side] = jnp.concatenate([part[n, row : row + 1, :] for n in range(1, 9)], axis=0)
        for end, n in ((0, 0), (1, 9)):
            ring_c[end, side] = jnp.broadcast_to(part[n, row : row + 1, :], (8, 128))

    around = []
    for n, (dx, dy) in enumerate(sides):
        a, b = (0 if dx < 0 else 1), (0 if dy < 0 else 1)
        if dy == 0:
            src, dst = ring_x.at[a], back_x.at[a]
        elif dx == 0:
            src, dst = ring_y.at[b], back_y.at[b]
        else:
            src, dst = ring_c.at[a, b], back_c.at[a, b]
        copy = pltpu.make_async_remote_copy(
            src_ref=src, dst_ref=dst, send_sem=ring_send.at[n], recv_sem=ring_recv.at[n],
            device_id=near(dx, dy), device_id_type=MESH,
        )
        copy.start()
        around.append(copy)

    for copy in first:
        copy.wait()
    tile_y[...] = sum_slots(red_g)

    second = []
    for s in range(1, ny):
        copy = pltpu.make_async_remote_copy(
            src_ref=tile_y, dst_ref=red_y.at[py],
            send_sem=red_send.at[1, s], recv_sem=red_recv.at[1, s],
            device_id=along_y(s), device_id_type=MESH,
        )
        copy.start()
        second.append(copy)
    red_y[py] = tile_y[...]

    for copy in around:
        copy.wait()
    for x in range(8):
        i = x + XOFF
        back = part[x + 1, 8:16, :]
        add_lo = back_y[1, x : x + 1, :] * myl
        add_hi = back_y[0, x : x + 1, :] * myh
        if x == 0:
            back = back + back_x[1] * mxl
            add_lo = add_lo + back_c[1, 1, 0:1, :] * (mxl * myl)
            add_hi = add_hi + back_c[1, 0, 0:1, :] * (mxl * myh)
        if x == 7:
            back = back + back_x[0] * mxh
            add_lo = add_lo + back_c[0, 1, 0:1, :] * (mxh * myl)
            add_hi = add_hi + back_c[0, 0, 0:1, :] * (mxh * myh)
        back = back + jnp.where(row8 == 0, add_lo, 0.0) + jnp.where(row8 == 7, add_hi, 0.0)
        smooth = smooth_at(g1, w0, i)[8:16]
        out_grad[x] = g1[i, 8:16, :] - TAU * smooth + back + TAU * upstream[x]

    for copy in second:
        copy.wait()
    tile_z[...] = sum_slots(red_y)
    third = []
    for s in range(1, nz):
        copy = pltpu.make_async_remote_copy(
            src_ref=tile_z, dst_ref=red_z.at[pz],
            send_sem=red_send.at[2, s], recv_sem=red_recv.at[2, s],
            device_id=along_z(s), device_id_type=MESH,
        )
        copy.start()
        third.append(copy)
    red_z[pz] = tile_z[...]
    for copy in third:
        copy.wait()
    tile_f[...] = sum_slots(red_z)
    fourth = []
    for s in range(1, 8):
        to, peer = in_group(s)
        copy = pltpu.make_async_remote_copy(
            src_ref=tile_f, dst_ref=final.at[me_g],
            send_sem=red_send.at[3, s], recv_sem=red_recv.at[3, s],
            device_id=peer, device_id_type=MESH,
        )
        copy.start()
        fourth.append(copy)
    final[me_g] = tile_f[...]
    for copy in fourth:
        copy.wait()

    scale = 1.0 / 2048.0
    whole = final[...].reshape(CH, 128) * scale
    turned = whole.T
    for k in range(2):
        out_w1[k] = whole[:, 64 * k : 64 * k + 27]
        out_w2[k] = turned[64 * k + 32 : 64 * k + 59, :]
        out_b[k : k + 1, :] = turned[64 * k + 27 : 64 * k + 28, :]


def sum_slots(store):
    total = store[0]
    for n in range(1, store.shape[0]):
        total = total + store[n]
    return total


def body(noisy, weights, filter_in, bias, filter_out, upstream):
    size_x, size_y = lax.axis_size("gx"), lax.axis_size("gy")
    field = pltpu.VMEM((LAYERS_X, ROWS, 128), F32)
    stack = pltpu.VMEM((LAYERS_X, SLAB, 128), BF16)
    vm = lambda *shape: pltpu.VMEM(shape, F32)
    vb = lambda *shape: pltpu.VMEM(shape, BF16)
    dma = lambda *shape: pltpu.SemaphoreType.DMA(shape)
    scratch = [
        vb(8, 32, 128), vb(8, 16, 128), vb(8, 16, 128), vb(2, 5, 32, 128), vb(2, LAYERS_X, 16, 128),
        field, field, field, field, field, field,
        stack, stack, stack, stack,
        vb(16 * CH, DEPTH), vb(12 * CH, DEPTH), vb(12 * CH, DEPTH), vb(8 * CH, DEPTH),
        vb(9 * ROWS, 16 * CH), vb(9 * ROWS, 12 * CH), vb(9 * ROWS, 8 * CH),
        vm(2, CH, 128), vm(2, 32, CH),
        vm(16, 9 * ROWS, 128), vm(12, 9 * ROWS, 128),
        vb(4, 8 * CH, 256), vm(4, 8 * CH, 256), vb(4, 8 * CH, 256), vb(4, 8 * CH, 256), vb(4, 8 * CH, 256),
        vm(2, 8, 128), vm(2, 8, 128), vm(2, 2, 8, 128), vm(2, 8, 128), vm(2, 8, 128), vm(2, 2, 8, 128), vm(10, ROWS, 128),
        vm(8, 8, 128), vm(8, 8, 128), vm(size_x // 4, 8, 128), vm(size_y // 2, 8, 128),
        vm(8, 128), vm(8, 128), vm(8, 128), vm(8, 8, 128),
        dma(8), dma(8), dma(8), dma(8), dma(4, 8), dma(4, 8),
    ]
    spec = pl.BlockSpec(memory_space=pltpu.VMEM)
    return pl.pallas_call(
        functools.partial(kernel, size_x, size_y),
        out_shape=(
            jax.ShapeDtypeStruct((8, 8, 128), F32),
            jax.ShapeDtypeStruct((2, CH, 27), F32),
            jax.ShapeDtypeStruct((2, 27, CH), F32),
            jax.ShapeDtypeStruct((2, CH), F32),
        ),
        in_specs=[spec] * 6,
        out_specs=(spec,) * 4,
        scratch_shapes=scratch,
        compiler_params=pltpu.CompilerParams(
            collective_id=0, has_side_effects=True, vmem_limit_bytes=48 * 1024 * 1024
        ),
    )(noisy, weights, filter_in, bias, filter_out, upstream)


def solution(mesh):
    return jax.shard_map(
        body,
        mesh=mesh,
        in_specs=(
            P("gx", "gy", None),
            P(None, "gx", "gy", None),
            P(),
            P(),
            P(),
            P("gx", "gy", None),
        ),
        out_specs=(P("gx", "gy", None), P(), P(), P()),
        check_vma=False,
    )
```

time: 292 us -> 58.9 us (0.20); the launches traced: 288 us -> 58.5 us
  blocking collectives: 114 us -> 0 us
  starting transfers between devices: 80.5 us -> 0 us
  Pallas kernels: 0 us -> 52.2 us
  local copies, waits for them, and re-layouts: 51.2 us -> 5.6 us
  waiting for transfers between devices: 19.2 us -> 0 us
  matrix products: 12.8 us -> 0 us
  other arithmetic: 7.75 us -> 0 us
    psum x1 -> x0, blocking collectives: 114 us -> none  [body(): g_in, g_out, g_bias = lax.psum((g_in, g_out, g_bias), ('gx', 'gy'))]
    ppermute x26 -> x0, starting transfers between devices: 80.5 us -> none  [the longest x12 49.9 us: padded_2(): before = lax.ppermute(last, axis, up)]
    pallas_call x0 -> x1, Pallas kernels: none -> 52.2 us  [body(): pl.pallas_call(functools.partial(kernel, size_x, size_y), out_shape=(jax....]
    another operation x181 -> x0, local copies, waits for them, and re-layouts: 37.5 us -> none  [the longest x179 36.9 us: stack_offsets(): return jnp.stack(parts, axis=-4)]
    ppermute x26 -> x0, waiting for transfers between devices: 19.2 us -> none  [the longest x12 19.1 us: padded_2(): after = lax.ppermute(leading, axis, down)]
    dot_general x11 -> x0, matrix products: 12.8 us -> none  [the longest x2 4.41 us: body(): jnp.einsum('jc,jxyz->cxyz', filter_out[k], shifted, preferred_element_typ...]
    slice x15 -> x0, local copies, waits for them, and re-layouts: 5.35 us -> none  [the longest x2 1.43 us: padded_2(): leading = lax.slice_in_dim(array, 0, width, axis=dim)]
    slice x5 -> x0, other arithmetic: 3.97 us -> none  [the longest x3 3.89 us: spread_total_sum(): total = total + padded[index, a0:a0 + n0, a1:a1 + n1, a2:a2 + n2]]
  transfers between devices with their start and end apart: 26 -> 0, of which waited for: 6 -> 0; matrix products, arithmetic and copies ran while one was open for 11% -> 0% of each run, Pallas kernels for 0% -> 0%
where the time goes in v1:
time: 58.9 us; the launch traced here: 58.5 us
  Pallas kernels  52.2 us (89%)
  local copies, waits for them, and re-layouts  5.6 us (10%)
  between operations  0.67 us (1%)
    pallas_call x1, Pallas kernels, body(): pl.pallas_call(functools.partial(kernel, size_x, size_y), out_shape=(jax....  52.2 us
    unnamed x12, local copies, waits for them, and re-layouts  4.28 us
    pallas_call x2, local copies, waits for them, and re-layouts, body(): pl.pallas_call(functools.partial(kernel, size_x, size_y), out_shape=(jax....  1.33 us

profile of v1, /device:TPU:1, one launch (start us, length us, event | category | flops | bytes accessed | tf_op | source)
XLA Modules:
  0.0 58.5 jit_solution(6155710330661631853)
XLA Ops:
  0.6 0.0 copy-start
  0.6 0.7 %copy.11.filter_out = bf16[2,27,64]{2,1,0:T(8,128)(2,1)S(1)} copy(bf16[2,27,64]{2,0,1:T(2,128)(2,1)} %param.10) | data formatting | bytes 13824 | tf_op args[4]
  1.4 0.0 copy-start.3
  1.4 0.8 %copy.10.filter_in = bf16[2,64,27]{2,1,0:T(8,128)(2,1)S(1)} copy(bf16[2,64,27]{1,0,2:T(2,128)(2,1)} %param.8) | data formatting | bytes 13824 | tf_op args[2]
  2.2 0.0 copy-done
  2.2 0.0 copy-done.3
  2.2 0.0 copy-start.1
  2.3 0.7 %copy-done.1 = f32[8,8,128]{2,1,0:T(8,128)S(1)} copy-done((f32[8,8,128]{2,1,0:T(8,128)S(1)}, f32[8,8,128]{2,1,0:T(8,128)}, u32[]{:S(2)}) %copy-start.1) | copy-done | bytes 32792
  3.0 0.0 copy-start.2
  3.0 0.8 %copy-done.2 = f32[8,8,128]{2,1,0:T(8,128)S(1)} copy-done((f32[8,8,128]{2,1,0:T(8,128)S(1)}, f32[8,8,128]{2,1,0:T(8,128)}, u32[]{:S(2)}) %copy-start.2) | copy-done | bytes 32792
  3.8 52.2 %shard_map.93 = (f32[8,8,128]{2,1,0:T(8,128)S(1)}, f32[2,64,27]{2,1,0:T(8,128)S(1)}, f32[2,27,64]{2,1,0:T(8,128)S(1)}, f32[2,64]{1,0:T(2,128)S(1)}) custom-call(f32[8,8,128]{2,1,0:T(8,128)S(1)} %copy-done.1, f32[2,8,8,128]{3,2,1,0:T(8,128)S(1)} %copy-done, bf16[2,64,27]{2,1,0:T(8,128)(2,1)S(1)} %copy.10.filter_in, f32[2,64]{1,0:T(2,128)S(1)} %copy-done.3, ...), custom_call_target="tpu_custom_call" | custom-call | tf_op jit(solution)/shard_map/pallas_call | solution.py:556
  56.0 0.7 %copy.12 = f32[2,64,27]{1,0,2:T(2,128)} copy(f32[2,64,27]{2,1,0:T(8,128)S(1)} %get-tuple-element.5) | data formatting | bytes 27648 | tf_op jit(solution)/shard_map/pallas_call | solution.py:556
  56.7 0.6 %copy.13 = f32[2,27,64]{2,0,1:T(2,128)} copy(f32[2,27,64]{2,1,0:T(8,128)S(1)} %get-tuple-element.6) | data formatting | bytes 27648 | tf_op jit(solution)/shard_map/pallas_call | solution.py:556
  57.3 0.6 %copy.16 = f32[8,8,128]{2,1,0:T(8,128)} copy(f32[8,8,128]{2,1,0:T(8,128)S(1)} %get-tuple-element.12) | data formatting | bytes 65536
  58.0 0.6 copy.17
Async XLA Ops:
  0.6 1.6 %copy-start = (f32[2,8,8,128]{3,2,1,0:T(8,128)S(1)}, f32[2,8,8,128]{3,2,1,0:T(8,128)}, u32[]{:S(2)}) copy-start(f32[2,8,8,128]{3,2,1,0:T(8,128)} %weights.1) | copy-start | bytes 196612
  1.4 0.8 %copy-start.3 = (f32[2,64]{1,0:T(2,128)S(1)}, f32[2,64]{1,0:T(2,128)}, u32[]{:S(2)}) copy-start(f32[2,64]{1,0:T(2,128)} %bias.1) | copy-start | bytes 1540
  2.2 0.8 %copy-start.1 = (f32[8,8,128]{2,1,0:T(8,128)S(1)}, f32[8,8,128]{2,1,0:T(8,128)}, u32[]{:S(2)}) copy-start(f32[8,8,128]{2,1,0:T(8,128)} %noisy.1) | copy-start | bytes 98308
  3.0 0.8 %copy-start.2 = (f32[8,8,128]{2,1,0:T(8,128)S(1)}, f32[8,8,128]{2,1,0:T(8,128)}, u32[]{:S(2)}) copy-start(f32[8,8,128]{2,1,0:T(8,128)} %upstream.1) | copy-start | bytes 98308

commit v2 on v1

--- a/solution.py
+++ b/solution.py
@@ -17,6 +17,8 @@
 LAYERS_X = 18
 SLAB = 80
 DEPTH = 3 * SLAB
+GROWS = 16
+GBASE = 4
 
 
 def iota(shape, axis):
@@ -64,8 +66,8 @@
 
 def split_rows(shape, axis):
     m = iota(shape, axis)
-    s = sum((m >= ROWS * n).astype(jnp.int32) for n in range(1, 9))
-    row = m - ROWS * s
+    s = sum((m >= GROWS * n).astype(jnp.int32) for n in range(1, 9))
+    row = m - GROWS * s + GBASE
     sx = (s >= 3).astype(jnp.int32) + (s >= 6).astype(jnp.int32)
     return sx, s - 3 * sx, row
 
@@ -118,7 +120,7 @@
 
 
 def fill_gather(out, weight, ys, sign, low, high):
-    shape = (9 * ROWS, 32)
+    shape = (9 * GROWS, 32)
     sx, sz, row = split_rows(shape, 0)
     base = 9 * sx + sz
     j = iota(shape, 1)
@@ -128,7 +130,7 @@
             step = (y + 9) - row if sign > 0 else row - (y + 7)
             hit = (step >= 0) & (step <= 2) & (j == base + 3 * step)
             part = one_hot(hit)
-            half = dot(part, weight) if sign > 0 else dot_nt(part, weight)
+            half = dot(part, weight)
             if y < 0:
                 half = half * low
             elif y > 7:
@@ -149,13 +151,14 @@
         part = None
         for sx in range(3):
             at = n + sx if sign > 0 else n + 2 - sx
-            lo = (3 * sx + sz) * ROWS
-            term = store[at, lo : lo + ROWS, :]
+            lo = (3 * sx + sz) * GROWS
+            term = store[at, lo : lo + GROWS, :]
             part = term if part is None else part + term
         if sz != 1:
             part = move_z(part, sign * (sz - 1))
         total = part if total is None else total + part
-    return total
+    pad = jnp.zeros((GBASE, 128), F32)
+    return jnp.concatenate([pad, total, pad], axis=0)
 
 
 def fold_rows(out):
@@ -197,8 +200,9 @@
 
 def kernel(
     size_x, size_y,
+    noisy_at, weights_at, filter_in_at, bias_at, filter_out_at, upstream_at,
+    out_grad, out_w1, out_w2, out_b,
     noisy, weights, filter_in, bias, filter_out, upstream,
-    out_grad, out_w1, out_w2, out_b,
     send_x, send_yl, send_yh, got_x, got_y,
     u0, g0, w0, w1, u1, g1,
     su0, ss1, su1, ss0,
@@ -207,7 +211,7 @@
     qbuf, pbuf, h0, d0, h1, dab1, dab0,
     ring_x, ring_y, ring_c, back_x, back_y, back_c, part,
     pack, red_g, red_y, red_z, tile_y, tile_z, tile_f, final,
-    halo_send, halo_recv, ring_send, ring_recv, red_send, red_recv,
+    fetch_sem, halo_send, halo_recv, ring_send, ring_recv, red_send, red_recv,
 ):
     gx, gy = lax.axis_index("gx"), lax.axis_index("gy")
     core, xlo, py = lax.rem(gx, 2), lax.rem(gx // 2, 2), gx // 4
@@ -229,19 +233,32 @@
     def along_z(step):
         return (gx, lax.rem(pz + step, nz) * 2 + xhi)
 
-    sides = [(dx, dy) for dx in (-1, 0, 1) for dy in (-1, 0, 1) if (dx, dy) != (0, 0)]
+    sides = [(-1, -1), (1, 1), (-1, 1), (1, -1), (0, -1), (0, 1), (-1, 0), (1, 0)]
+    far_first = (4, 3, 5, 2, 6, 1, 7)
     barrier = pltpu.get_barrier_semaphore()
     peers = [near(*side) for side in sides] + [in_group(s)[1] for s in range(1, 8)]
     peers += [along_y(s) for s in range(1, ny)] + [along_z(s) for s in range(1, nz)]
     for peer in peers:
         pl.semaphore_signal(barrier, inc=1, device_id=peer, device_id_type=MESH)
 
+    fetched = [
+        pltpu.make_async_copy(src, dst, fetch_sem.at[n])
+        for n, (src, dst) in enumerate((
+            (noisy_at, noisy), (upstream_at, upstream), (weights_at, weights),
+            (filter_in_at, filter_in), (filter_out_at, filter_out), (bias_at, bias),
+        ))
+    ]
+    for copy in fetched:
+        copy.start()
+
     mxl = jnp.where(gx > 0, 1.0, 0.0).astype(F32)
     mxh = jnp.where(gx < size_x - 1, 1.0, 0.0).astype(F32)
     myl = jnp.where(gy > 0, 1.0, 0.0).astype(F32)
     myh = jnp.where(gy < size_y - 1, 1.0, 0.0).astype(F32)
 
     row8 = iota((8, 128), 0)
+    for copy in fetched[:3]:
+        copy.wait()
     for x in range(8):
         u, g, wa, wb = noisy[x], upstream[x], weights[0, x], weights[1, x]
         send_x[x] = jnp.concatenate([u, g, wa, wb], axis=0).astype(BF16)
@@ -271,24 +288,28 @@
         halo.append(copy)
 
     eye = iota((CH, CH), 0) == iota((CH, CH), 1)
+    for copy in fetched[3:]:
+        copy.wait()
     pad_in[...] = jnp.zeros_like(pad_in)
     pad_out[...] = jnp.zeros_like(pad_out)
+    whole_in, whole_out = filter_in[...].astype(F32), filter_out[...].astype(F32)
     cols = []
     for k in range(2):
-        pad_in[k, :, 0:27] = filter_in[k].astype(F32)
-        pad_out[k, 0:27, :] = filter_out[k].astype(F32)
+        pad_in[k, 0:27, :] = whole_in[:, k, :]
+        pad_out[k, 0:27, :] = whole_out[:, k, :]
         spread = jnp.broadcast_to(bias[k : k + 1, :], (CH, CH))
         cols.append(jnp.sum(jnp.where(eye, spread, 0.0), axis=1, keepdims=True))
-    win = [pad_in[k, :, 0:32].astype(BF16) for k in range(2)]
+    win_t = [pad_in[k].astype(BF16) for k in range(2)]
     wout = [pad_out[k].astype(BF16) for k in range(2)]
+    win = [dot_nt(one_hot(eye), win_t[k]).astype(BF16) for k in range(2)]
     wout_t = [dot_nt(one_hot(eye), wout[k]).astype(BF16) for k in range(2)]
     fill_patch(t1a, win[0], cols[0], range(-4, 12))
     fill_gather(toa, wout[0], range(-4, 12), 1, myl, myh)
     fill_patch(t1b, win[1], cols[1], range(-2, 10))
     fill_spread(t2b, wout_t[1], range(-2, 10))
-    fill_gather(t3b, win[1], range(-2, 10), -1, myl, myh)
+    fill_gather(t3b, win_t[1], range(-2, 10), -1, myl, myh)
     fill_spread(t2a, wout_t[0], range(0, 8))
-    fill_gather(t3a, win[0], range(0, 8), -1, myl, myh)
+    fill_gather(t3a, win_t[0], range(0, 8), -1, myl, myh)
 
     for copy in halo:
         copy.wait()
@@ -324,23 +345,28 @@
 
     def forward(p, keep):
         i = 1 + 2 * p
-        half = dot(t1a[...], pair_of(su0, i))
-        t = jnp.tanh(half)
-        h = half + half * t
-        hb = h.astype(BF16)
-        if keep:
-            tile = slice(4 * CH, 12 * CH)
-            h0[p - 2] = hb[tile]
-            d0[p - 2] = (1.0 + t[tile]) + (h[tile] - h[tile] * t[tile])
-        q = dot(toa[...], hb)
+        rhs = pair_of(su0, i)
+        q = None
+        for m in range(4):
+            cut = slice(4 * CH * m, 4 * CH * (m + 1))
+            half = dot(t1a[cut, :], rhs)
+            t = jnp.tanh(half)
+            h = half + half * t
+            hb = h.astype(BF16)
+            if keep and m in (1, 2):
+                own = slice(4 * CH * (m - 1), 4 * CH * m)
+                h0[p - 2, own, :] = hb
+                d0[p - 2, own, :] = (1.0 + t) + (h - h * t)
+            term = dot(toa[:, cut], hb)
+            q = term if q is None else q + term
         qbuf[2 * p] = q[:, 0:128] * x_mask(i)
         qbuf[2 * p + 1] = q[:, 128:256] * x_mask(i + 1)
 
-    @pl.loop(0, 4)
+    @pl.loop(0, 4, unroll=2)
     def _(n):
         forward(jnp.where(n < 2, n, n + 4), False)
 
-    @pl.loop(2, 6)
+    @pl.loop(2, 6, unroll=2)
     def _(p):
         forward(p, True)
 
@@ -356,26 +382,37 @@
 
     def middle(p, keep):
         i = 3 + 2 * p
-        half = dot(t1b[...], pair_of(su1, i))
-        dh = dot(t2b[...], pair_of(ss1, i))
-        t = jnp.tanh(half)
-        h = half + half * t
-        dab = (dh * ((1.0 + t) + (h - h * t))).astype(BF16)
-        if keep:
-            tile = slice(2 * CH, 10 * CH)
-            h1[p - 1] = h[tile].astype(BF16)
-            dab1[p - 1] = dab[tile]
-        q = dot(t3b[...], dab)
+        rhs_u, rhs_s = pair_of(su1, i), pair_of(ss1, i)
+        q = None
+        for first, last in ((0, 2), (2, 6), (6, 10), (10, 12)):
+            cut = slice(CH * first, CH * last)
+            half = dot(t1b[cut, :], rhs_u)
+            dh = dot(t2b[cut, :], rhs_s)
+            t = jnp.tanh(half)
+            h = half + half * t
+            dab = (dh * ((1.0 + t) + (h - h * t))).astype(BF16)
+            if keep and last - first == 4:
+                own = slice(CH * (first - 2), CH * (last - 2))
+                h1[p - 1, own, :] = h.astype(BF16)
+                dab1[p - 1, own, :] = dab
+            term = dot(t3b[:, cut], dab)
+            q = term if q is None else q + term
         pbuf[2 * p] = q[:, 0:128] * x_mask(i)
         pbuf[2 * p + 1] = q[:, 128:256] * x_mask(i + 1)
 
-    @pl.loop(0, 2)
+    @pl.loop(0, 2, unroll=2)
     def _(n):
         middle(n * 5, False)
 
-    @pl.loop(1, 5)
+    @pl.loop(1, 5, unroll=2)
     def _(p):
         middle(p, True)
+
+    def beside(store):
+        return jnp.concatenate([store[p] for p in range(4)], axis=1)
+
+    sums = packed_sums(dot_nt(beside(h1), layers_beside(ss1)), 1, False)
+    sums = sums + packed_sums(dot_nt(beside(dab1), layers_beside(su1)), 1, True)
 
     for i in range(4, 14):
         g = g0[i]
@@ -388,23 +425,18 @@
         g1[i] = v
         ss0[i] = slab_of(-TAU * v)
 
-    @pl.loop(0, 4)
+    @pl.loop(0, 4, unroll=4)
     def _(p):
         dh = dot(t2a[...], pair_of(ss0, XOFF + 2 * p))
         dab0[p] = (dh * d0[p]).astype(BF16)
 
-    def beside(store):
-        return jnp.concatenate([store[p] for p in range(4)], axis=1)
-
-    sums = packed_sums(dot_nt(beside(h0), layers_beside(ss0)), 0, False)
+    sums = sums + packed_sums(dot_nt(beside(h0), layers_beside(ss0)), 0, False)
     sums = sums + packed_sums(dot_nt(beside(dab0), layers_beside(su0)), 0, True)
-    sums = sums + packed_sums(dot_nt(beside(h1), layers_beside(ss1)), 1, False)
-    sums = sums + packed_sums(dot_nt(beside(dab1), layers_beside(su1)), 1, True)
     for n in range(8):
         pack[n] = sums[8 * n : 8 * n + 8]
 
     first = []
-    for s in range(1, 8):
+    for s in far_first:
         to, peer = in_group(s)
         copy = pltpu.make_async_remote_copy(
             src_ref=pack.at[to], dst_ref=red_g.at[me_g],
@@ -420,7 +452,7 @@
     pbuf[10] = jnp.zeros_like(pbuf[0])
     pbuf[11] = jnp.zeros_like(pbuf[0])
 
-    @pl.loop(0, 4)
+    @pl.loop(0, 4, unroll=2)
     def _(p):
         q = dot(t3a[...], dab0[p])
         pbuf[2 * p + 2] = q[:, 0:128]
@@ -456,7 +488,7 @@
     tile_y[...] = sum_slots(red_g)
 
     second = []
-    for s in range(1, ny):
+    for s in sorted(range(1, ny), key=lambda s: -min(s, ny - s)):
         copy = pltpu.make_async_remote_copy(
             src_ref=tile_y, dst_ref=red_y.at[py],
             send_sem=red_send.at[1, s], recv_sem=red_recv.at[1, s],
@@ -489,7 +521,7 @@
         copy.wait()
     tile_z[...] = sum_slots(red_y)
     third = []
-    for s in range(1, nz):
+    for s in sorted(range(1, nz), key=lambda s: -min(s, nz - s)):
         copy = pltpu.make_async_remote_copy(
             src_ref=tile_z, dst_ref=red_z.at[pz],
             send_sem=red_send.at[2, s], recv_sem=red_recv.at[2, s],
@@ -502,7 +534,7 @@
         copy.wait()
     tile_f[...] = sum_slots(red_z)
     fourth = []
-    for s in range(1, 8):
+    for s in far_first:
         to, peer = in_group(s)
         copy = pltpu.make_async_remote_copy(
             src_ref=tile_f, dst_ref=final.at[me_g],
@@ -519,8 +551,8 @@
     whole = final[...].reshape(CH, 128) * scale
     turned = whole.T
     for k in range(2):
-        out_w1[k] = whole[:, 64 * k : 64 * k + 27]
-        out_w2[k] = turned[64 * k + 32 : 64 * k + 59, :]
+        out_w1[:, k, :] = turned[64 * k : 64 * k + 27, :]
+        out_w2[:, k, :] = turned[64 * k + 32 : 64 * k + 59, :]
         out_b[k : k + 1, :] = turned[64 * k + 27 : 64 * k + 28, :]
 
 
@@ -529,6 +561,15 @@
     for n in range(1, store.shape[0]):
         total = total + store[n]
     return total
+
+
+def hand_over(*refs):
+    srcs, dsts, sems = refs[:4], refs[4:8], refs[8]
+    copies = [pltpu.make_async_copy(s, d, sems.at[n]) for n, (s, d) in enumerate(zip(srcs, dsts))]
+    for copy in copies:
+        copy.start()
+    for copy in copies:
+        copy.wait()
 
 
 def body(noisy, weights, filter_in, bias, filter_out, upstream):
@@ -539,35 +580,50 @@
     vb = lambda *shape: pltpu.VMEM(shape, BF16)
     dma = lambda *shape: pltpu.SemaphoreType.DMA(shape)
     scratch = [
+        vm(8, 8, 128), vm(2, 8, 8, 128), vb(27, 2, CH), vm(2, CH), vb(27, 2, CH), vm(8, 8, 128),
         vb(8, 32, 128), vb(8, 16, 128), vb(8, 16, 128), vb(2, 5, 32, 128), vb(2, LAYERS_X, 16, 128),
         field, field, field, field, field, field,
         stack, stack, stack, stack,
         vb(16 * CH, DEPTH), vb(12 * CH, DEPTH), vb(12 * CH, DEPTH), vb(8 * CH, DEPTH),
-        vb(9 * ROWS, 16 * CH), vb(9 * ROWS, 12 * CH), vb(9 * ROWS, 8 * CH),
-        vm(2, CH, 128), vm(2, 32, CH),
-        vm(16, 9 * ROWS, 128), vm(12, 9 * ROWS, 128),
+        vb(9 * GROWS, 16 * CH), vb(9 * GROWS, 12 * CH), vb(9 * GROWS, 8 * CH),
+        vm(2, 32, CH), vm(2, 32, CH),
+        vm(16, 9 * GROWS, 128), vm(12, 9 * GROWS, 128),
         vb(4, 8 * CH, 256), vm(4, 8 * CH, 256), vb(4, 8 * CH, 256), vb(4, 8 * CH, 256), vb(4, 8 * CH, 256),
         vm(2, 8, 128), vm(2, 8, 128), vm(2, 2, 8, 128), vm(2, 8, 128), vm(2, 8, 128), vm(2, 2, 8, 128), vm(10, ROWS, 128),
         vm(8, 8, 128), vm(8, 8, 128), vm(size_x // 4, 8, 128), vm(size_y // 2, 8, 128),
         vm(8, 128), vm(8, 128), vm(8, 128), vm(8, 8, 128),
-        dma(8), dma(8), dma(8), dma(8), dma(4, 8), dma(4, 8),
+        dma(6), dma(8), dma(8), dma(8), dma(8), dma(4, 8), dma(4, 8),
     ]
     spec = pl.BlockSpec(memory_space=pltpu.VMEM)
-    return pl.pallas_call(
+    far = pl.BlockSpec(memory_space=pltpu.HBM)
+    shapes = (
+        jax.ShapeDtypeStruct((8, 8, 128), F32),
+        jax.ShapeDtypeStruct((27, 2, CH), F32),
+        jax.ShapeDtypeStruct((27, 2, CH), F32),
+        jax.ShapeDtypeStruct((2, CH), F32),
+    )
+    results = pl.pallas_call(
         functools.partial(kernel, size_x, size_y),
-        out_shape=(
-            jax.ShapeDtypeStruct((8, 8, 128), F32),
-            jax.ShapeDtypeStruct((2, CH, 27), F32),
-            jax.ShapeDtypeStruct((2, 27, CH), F32),
-            jax.ShapeDtypeStruct((2, CH), F32),
-        ),
-        in_specs=[spec] * 6,
+        out_shape=shapes,
+        in_specs=[far] * 6,
         out_specs=(spec,) * 4,
         scratch_shapes=scratch,
         compiler_params=pltpu.CompilerParams(
-            collective_id=0, has_side_effects=True, vmem_limit_bytes=48 * 1024 * 1024
+            collective_id=0, has_side_effects=True, vmem_limit_bytes=60 * 1024 * 1024
         ),
-    )(noisy, weights, filter_in, bias, filter_out, upstream)
+    )(
+        noisy, weights, jnp.transpose(filter_in, (2, 0, 1)), bias,
+        jnp.transpose(filter_out, (1, 0, 2)), upstream,
+    )
+    grad, w1, w2, b = pl.pallas_call(
+        hand_over,
+        out_shape=shapes,
+        in_specs=[far] * 4,
+        out_specs=(far,) * 4,
+        scratch_shapes=[pltpu.SemaphoreType.DMA((4,))],
+        compiler_params=pltpu.CompilerParams(vmem_limit_bytes=60 * 1024 * 1024),
+    )(*results)
+    return grad, jnp.transpose(w1, (1, 2, 0)), jnp.transpose(w2, (1, 0, 2)), b
 
 
 def solution(mesh):

time: 58.9 us -> 55.5 us (0.942)
  local copies, waits for them, and re-layouts: 5.6 us -> 0 us
  Pallas kernels: 52.2 us -> 54.7 us
    unnamed x12 -> x0, local copies, waits for them, and re-layouts: 4.28 us -> none
    pallas_call x1 -> x2, Pallas kernels: 52.2 us -> 54.7 us  [the longest x1 50.9 us: body(): pl.pallas_call(functools.partial(kernel, size_x, size_y), out_shape=shape...]
    pallas_call x2 -> x0, local copies, waits for them, and re-layouts: 1.33 us -> none  [body(): pl.pallas_call(functools.partial(kernel, size_x, size_y), out_shape=(jax....]
where the time goes in v2:
time: 55.5 us; the launch traced here: 55.4 us
  Pallas kernels  54.7 us (99%)
  between operations  0.64 us (1%)
    pallas_call x1, Pallas kernels, body(): pl.pallas_call(functools.partial(kernel, size_x, size_y), out_shape=shape...  50.9 us
    pallas_call x1, Pallas kernels, body(): pl.pallas_call(hand_over, out_shape=shapes, in_specs=[far] * 4, out_specs...  3.84 us

profile of v2, /device:TPU:1, one launch (start us, length us, event | category | flops | bytes accessed | tf_op | source)
XLA Modules:
  0.0 55.4 jit_solution(1161348396548834306)
XLA Ops:
  0.6 50.9 %shard_map.93 = (f32[8,8,128]{2,1,0:T(8,128)}, f32[27,2,64]{2,1,0:T(2,128)}, f32[27,2,64]{2,1,0:T(2,128)}, f32[2,64]{1,0:T(2,128)}) custom-call(f32[8,8,128]{2,1,0:T(8,128)} %noisy_at.1, f32[2,8,8,128]{3,2,1,0:T(8,128)} %weights_at.1, bf16[27,2,64]{2,1,0:T(2,128)(2,1)} %bitcast.4, f32[2,64]{1,0:T(2,128)} %bias_at.1, bf16[27,2,64]{2,1,0:T(2,128)(2,1)} %bitcast.5, ...), custom_call_target="tpu_custom_call" | custom-call | tf_op jit(solution)/shard_map/pallas_call | solution.py:605
  51.5 3.8 %shard_map.94 = (f32[8,8,128]{2,1,0:T(8,128)}, f32[27,2,64]{2,1,0:T(2,128)}, f32[27,2,64]{2,1,0:T(2,128)}, f32[2,64]{1,0:T(2,128)}) custom-call(f32[8,8,128]{2,1,0:T(8,128)} %get-tuple-element.12.refs_0_, f32[27,2,64]{2,1,0:T(2,128)} %get-tuple-element.13.refs_1_, f32[27,2,64]{2,1,0:T(2,128)} %get-tuple-element.14.refs_2_, f32[2,64]{1,0:T(2,128)} %get-tuple-element.15.refs_3_), custom_call_target="tpu_custom_call" | custom-call | tf_op jit(solution)/shard_map/pallas_call | solution.py:618

commit v3 on v2

--- a/solution.py
+++ b/solution.py
@@ -344,6 +344,7 @@
         return jnp.where(i < XOFF, mxl, jnp.where(i >= XOFF + 8, mxh, 1.0))
 
     def forward(p, keep):
+        slot = jnp.where(p < 6, p - 2, 4)
         i = 1 + 2 * p
         rhs = pair_of(su0, i)
         q = None
@@ -355,32 +356,33 @@
             hb = h.astype(BF16)
             if keep and m in (1, 2):
                 own = slice(4 * CH * (m - 1), 4 * CH * m)
-                h0[p - 2, own, :] = hb
-                d0[p - 2, own, :] = (1.0 + t) + (h - h * t)
+                h0[slot, own, :] = hb
+                d0[slot, own, :] = (1.0 + t) + (h - h * t)
             term = dot(toa[:, cut], hb)
             q = term if q is None else q + term
         qbuf[2 * p] = q[:, 0:128] * x_mask(i)
         qbuf[2 * p + 1] = q[:, 128:256] * x_mask(i + 1)
 
-    @pl.loop(0, 4, unroll=2)
-    def _(n):
-        forward(jnp.where(n < 2, n, n + 4), False)
-
-    @pl.loop(2, 6, unroll=2)
+    def iterate(n):
+        i = n + 2
+        learned = gather_sum(qbuf, n, 1)
+        v = u0[i] - TAU * (smooth_at(u0, w0, i) + learned)
+        su1[i] = slab_of(v * (inside_y * x_mask(i)))
+
+    @pl.loop(0, 2, unroll=2)
     def _(p):
+        forward(p, False)
+
+    @pl.loop(2, 8, unroll=2)
+    def _(p):
+        iterate(2 * p - 4)
+        iterate(2 * p - 3)
         forward(p, True)
 
-    for i in range(2, 16):
-        learned = gather_sum(qbuf, i - 2, 1)
-        v = u0[i] - TAU * (smooth_at(u0, w0, i) + learned)
-        v = v * inside_y
-        if i < XOFF:
-            v = v * mxl
-        elif i >= XOFF + 8:
-            v = v * mxh
-        su1[i] = slab_of(v)
-
-    def middle(p, keep):
+    iterate(12)
+    iterate(13)
+
+    def middle(p, slot):
         i = 3 + 2 * p
         rhs_u, rhs_s = pair_of(su1, i), pair_of(ss1, i)
         q = None
@@ -391,39 +393,41 @@
             t = jnp.tanh(half)
             h = half + half * t
             dab = (dh * ((1.0 + t) + (h - h * t))).astype(BF16)
-            if keep and last - first == 4:
+            if last - first == 4:
                 own = slice(CH * (first - 2), CH * (last - 2))
-                h1[p - 1, own, :] = h.astype(BF16)
-                dab1[p - 1, own, :] = dab
+                h1[slot, own, :] = h.astype(BF16)
+                dab1[slot, own, :] = dab
             term = dot(t3b[:, cut], dab)
             q = term if q is None else q + term
         pbuf[2 * p] = q[:, 0:128] * x_mask(i)
         pbuf[2 * p + 1] = q[:, 128:256] * x_mask(i + 1)
 
+    def cotangent(n):
+        i = n + 4
+        g = g0[i]
+        v = g - TAU * (g + smooth_at(g0, w1, i)) + gather_sum(pbuf, n, -1)
+        v = v * (inside_y * x_mask(i))
+        g1[i] = v
+        ss0[i] = slab_of(-TAU * v)
+
     @pl.loop(0, 2, unroll=2)
-    def _(n):
-        middle(n * 5, False)
-
-    @pl.loop(1, 5, unroll=2)
     def _(p):
-        middle(p, True)
+        middle(p, jnp.where(p > 0, 0, 4))
+
+    @pl.loop(2, 6, unroll=2)
+    def _(p):
+        cotangent(2 * p - 4)
+        cotangent(2 * p - 3)
+        middle(p, jnp.where(p < 5, p - 1, 4))
+
+    cotangent(8)
+    cotangent(9)
 
     def beside(store):
         return jnp.concatenate([store[p] for p in range(4)], axis=1)
 
     sums = packed_sums(dot_nt(beside(h1), layers_beside(ss1)), 1, False)
     sums = sums + packed_sums(dot_nt(beside(dab1), layers_beside(su1)), 1, True)
-
-    for i in range(4, 14):
-        g = g0[i]
-        v = g - TAU * (g + smooth_at(g0, w1, i)) + gather_sum(pbuf, i - 4, -1)
-        v = v * inside_y
-        if i < XOFF:
-            v = v * mxl
-        elif i >= XOFF + 8:
-            v = v * mxh
-        g1[i] = v
-        ss0[i] = slab_of(-TAU * v)
 
     @pl.loop(0, 4, unroll=4)
     def _(p):
@@ -563,15 +567,6 @@
     return total
 
 
-def hand_over(*refs):
-    srcs, dsts, sems = refs[:4], refs[4:8], refs[8]
-    copies = [pltpu.make_async_copy(s, d, sems.at[n]) for n, (s, d) in enumerate(zip(srcs, dsts))]
-    for copy in copies:
-        copy.start()
-    for copy in copies:
-        copy.wait()
-
-
 def body(noisy, weights, filter_in, bias, filter_out, upstream):
     size_x, size_y = lax.axis_size("gx"), lax.axis_size("gy")
     field = pltpu.VMEM((LAYERS_X, ROWS, 128), F32)
@@ -588,7 +583,7 @@
         vb(9 * GROWS, 16 * CH), vb(9 * GROWS, 12 * CH), vb(9 * GROWS, 8 * CH),
         vm(2, 32, CH), vm(2, 32, CH),
         vm(16, 9 * GROWS, 128), vm(12, 9 * GROWS, 128),
-        vb(4, 8 * CH, 256), vm(4, 8 * CH, 256), vb(4, 8 * CH, 256), vb(4, 8 * CH, 256), vb(4, 8 * CH, 256),
+        vb(5, 8 * CH, 256), vm(5, 8 * CH, 256), vb(5, 8 * CH, 256), vb(5, 8 * CH, 256), vb(4, 8 * CH, 256),
         vm(2, 8, 128), vm(2, 8, 128), vm(2, 2, 8, 128), vm(2, 8, 128), vm(2, 8, 128), vm(2, 2, 8, 128), vm(10, ROWS, 128),
         vm(8, 8, 128), vm(8, 8, 128), vm(size_x // 4, 8, 128), vm(size_y // 2, 8, 128),
         vm(8, 128), vm(8, 128), vm(8, 128), vm(8, 8, 128),
@@ -596,13 +591,8 @@
     ]
     spec = pl.BlockSpec(memory_space=pltpu.VMEM)
     far = pl.BlockSpec(memory_space=pltpu.HBM)
-    shapes = (
-        jax.ShapeDtypeStruct((8, 8, 128), F32),
-        jax.ShapeDtypeStruct((27, 2, CH), F32),
-        jax.ShapeDtypeStruct((27, 2, CH), F32),
-        jax.ShapeDtypeStruct((2, CH), F32),
-    )
-    results = pl.pallas_call(
+    shapes = (vm(8, 8, 128), vm(27, 2, CH), vm(27, 2, CH), vm(2, CH))
+    grad, w1, w2, b = pl.pallas_call(
         functools.partial(kernel, size_x, size_y),
         out_shape=shapes,
         in_specs=[far] * 6,
@@ -615,14 +605,6 @@
         noisy, weights, jnp.transpose(filter_in, (2, 0, 1)), bias,
         jnp.transpose(filter_out, (1, 0, 2)), upstream,
     )
-    grad, w1, w2, b = pl.pallas_call(
-        hand_over,
-        out_shape=shapes,
-        in_specs=[far] * 4,
-        out_specs=(far,) * 4,
-        scratch_shapes=[pltpu.SemaphoreType.DMA((4,))],
-        compiler_params=pltpu.CompilerParams(vmem_limit_bytes=60 * 1024 * 1024),
-    )(*results)
     return grad, jnp.transpose(w1, (1, 2, 0)), jnp.transpose(w2, (1, 0, 2)), b
 
 

time: 55.5 us -> 53.1 us (0.957)
  Pallas kernels: 54.7 us -> 49.9 us
  local copies, waits for them, and re-layouts: 0 us -> 2.4 us
    pallas_call x1 -> x0, Pallas kernels: 3.84 us -> none  [body(): pl.pallas_call(hand_over, out_shape=shapes, in_specs=[far] * 4, out_specs...]
    unnamed x0 -> x4, local copies, waits for them, and re-layouts: none -> 2.4 us
    pallas_call x1, Pallas kernels: 50.9 us -> 49.9 us  [body(): pl.pallas_call(functools.partial(kernel, size_x, size_y), out_shape=shape...]
where the time goes in v3:
time: 53.1 us; the launch traced here: 53 us
  Pallas kernels  49.9 us (94%)
  local copies, waits for them, and re-layouts  2.4 us (5%)
  between operations  0.64 us (1%)
    pallas_call x1, Pallas kernels, body(): pl.pallas_call(functools.partial(kernel, size_x, size_y), out_shape=shape...  49.9 us
    unnamed x4, local copies, waits for them, and re-layouts  2.4 us

profile of v3, /device:TPU:1, one launch (start us, length us, event | category | flops | bytes accessed | tf_op | source)
XLA Modules:
  0.0 53.0 jit_solution(15178919183743291287)
XLA Ops:
  0.6 49.9 %shard_map.93 = (f32[8,8,128]{2,1,0:T(8,128)S(1)}, f32[27,2,64]{2,1,0:T(2,128)S(1)}, f32[27,2,64]{2,1,0:T(2,128)S(1)}, f32[2,64]{1,0:T(2,128)S(1)}) custom-call(f32[8,8,128]{2,1,0:T(8,128)} %noisy_at.1, f32[2,8,8,128]{3,2,1,0:T(8,128)} %weights_at.1, bf16[27,2,64]{2,1,0:T(2,128)(2,1)} %bitcast.6, f32[2,64]{1,0:T(2,128)} %bias_at.1, ...), custom_call_target="tpu_custom_call" | custom-call | tf_op jit(solution)/shard_map/pallas_call | solution.py:595
  50.6 0.6 %copy.14 = f32[8,8,128]{2,1,0:T(8,128)} copy(f32[8,8,128]{2,1,0:T(8,128)S(1)} %get-tuple-element.12) | data formatting | bytes 65536
  51.2 0.6 %copy.15 = f32[2,64,27]{1,0,2:T(2,128)} copy(f32[2,64,27]{1,0,2:T(2,128)S(1)} %bitcast.5) | data formatting | bytes 27648
  51.8 0.6 %copy.17 = f32[2,64]{1,0:T(2,128)} copy(f32[2,64]{1,0:T(2,128)S(1)} %get-tuple-element.15) | data formatting | bytes 1024
  52.4 0.6 %copy.16 = f32[2,27,64]{2,0,1:T(2,128)} copy(f32[2,27,64]{2,0,1:T(2,128)S(1)} %bitcast.4) | data formatting | bytes 27648

commit v4 on v3

--- a/solution.py
+++ b/solution.py
@@ -185,9 +185,8 @@
     return one_hot(ok & (lane == 64 * layer + 32 + j))
 
 
-def packed_sums(out, layer, first):
+def packed_sums(out, pick):
     folded = fold_rows(out)
-    pick = pick_columns(layer, first)
     high, mid, low = thirds(folded)
     return dot(high, pick) + dot(mid, pick) + dot(low, pick)
 
@@ -201,13 +200,13 @@
 def kernel(
     size_x, size_y,
     noisy_at, weights_at, filter_in_at, bias_at, filter_out_at, upstream_at,
-    out_grad, out_w1, out_w2, out_b,
+    out_grad, out_p,
     noisy, weights, filter_in, bias, filter_out, upstream,
     send_x, send_yl, send_yh, got_x, got_y,
     u0, g0, w0, w1, u1, g1,
     su0, ss1, su1, ss0,
     t1a, t1b, t2b, t2a, toa, t3b, t3a,
-    pad_in, pad_out,
+    pad_in, pad_out, picks,
     qbuf, pbuf, h0, d0, h1, dab1, dab0,
     ring_x, ring_y, ring_c, back_x, back_y, back_c, part,
     pack, red_g, red_y, red_z, tile_y, tile_z, tile_f, final,
@@ -238,9 +237,8 @@
     barrier = pltpu.get_barrier_semaphore()
     peers = [near(*side) for side in sides] + [in_group(s)[1] for s in range(1, 8)]
     peers += [along_y(s) for s in range(1, ny)] + [along_z(s) for s in range(1, nz)]
-    for peer in peers:
+    for peer in peers[: len(sides)]:
         pl.semaphore_signal(barrier, inc=1, device_id=peer, device_id_type=MESH)
-
     fetched = [
         pltpu.make_async_copy(src, dst, fetch_sem.at[n])
         for n, (src, dst) in enumerate((
@@ -250,6 +248,8 @@
     ]
     for copy in fetched:
         copy.start()
+    for peer in peers[len(sides) :]:
+        pl.semaphore_signal(barrier, inc=1, device_id=peer, device_id_type=MESH)
 
     mxl = jnp.where(gx > 0, 1.0, 0.0).astype(F32)
     mxh = jnp.where(gx < size_x - 1, 1.0, 0.0).astype(F32)
@@ -260,7 +260,7 @@
     for copy in fetched[:3]:
         copy.wait()
     for x in range(8):
-        u, g, wa, wb = noisy[x], upstream[x], weights[0, x], weights[1, x]
+        u, g, wa, wb = noisy[x], -TAU * upstream[x], weights[0, x], weights[1, x]
         send_x[x] = jnp.concatenate([u, g, wa, wb], axis=0).astype(BF16)
         top = jnp.where(row8 < 5, pltpu.roll(u, 5, 0), g)
         low = jnp.where(row8 < 4, pltpu.roll(wa, 4, 0), pltpu.roll(wb, 6, 0))
@@ -303,6 +303,8 @@
     wout = [pad_out[k].astype(BF16) for k in range(2)]
     win = [dot_nt(one_hot(eye), win_t[k]).astype(BF16) for k in range(2)]
     wout_t = [dot_nt(one_hot(eye), wout[k]).astype(BF16) for k in range(2)]
+    for n in range(4):
+        picks[n] = pick_columns(n // 2, n % 2 == 1)
     fill_patch(t1a, win[0], cols[0], range(-4, 12))
     fill_gather(toa, wout[0], range(-4, 12), 1, myl, myh)
     fill_patch(t1b, win[1], cols[1], range(-2, 10))
@@ -330,9 +332,12 @@
         su0[i] = slab_of(u)
         w0[i] = jnp.concatenate([pltpu.roll(lo_b, 4, 0), rows[16:24], hi_b], axis=0)
         if 2 <= i < 16:
-            g = jnp.concatenate([lo_t, rows[8:16], pltpu.roll(hi_t, 3, 0)], axis=0)
-            g0[i] = g
-            ss1[i] = slab_of(-TAU * g)
+            own = XOFF <= i < XOFF + 8
+            mid = rows[8:16]
+            lo_g, hi_g = lo_t, pltpu.roll(hi_t, 3, 0)
+            ss1[i] = slab_of(jnp.concatenate([lo_g, -TAU * mid if own else mid, hi_g], axis=0))
+            back = -1.0 / TAU
+            g0[i] = jnp.concatenate([lo_g * back, mid if own else mid * back, hi_g * back], axis=0)
             w1[i] = jnp.concatenate(
                 [pltpu.roll(lo_b, 2, 0), rows[24:32], pltpu.roll(hi_b, 4, 0)], axis=0
             )
@@ -426,30 +431,30 @@
     def beside(store):
         return jnp.concatenate([store[p] for p in range(4)], axis=1)
 
-    sums = packed_sums(dot_nt(beside(h1), layers_beside(ss1)), 1, False)
-    sums = sums + packed_sums(dot_nt(beside(dab1), layers_beside(su1)), 1, True)
+    sums = packed_sums(dot_nt(beside(h1), layers_beside(ss1)), picks[2])
+    sums = sums + packed_sums(dot_nt(beside(dab1), layers_beside(su1)), picks[3])
 
     @pl.loop(0, 4, unroll=4)
     def _(p):
         dh = dot(t2a[...], pair_of(ss0, XOFF + 2 * p))
         dab0[p] = (dh * d0[p]).astype(BF16)
 
-    sums = sums + packed_sums(dot_nt(beside(h0), layers_beside(ss0)), 0, False)
-    sums = sums + packed_sums(dot_nt(beside(dab0), layers_beside(su0)), 0, True)
-    for n in range(8):
-        pack[n] = sums[8 * n : 8 * n + 8]
+    sums = sums + packed_sums(dot_nt(beside(h0), layers_beside(ss0)), picks[0])
+    sums = sums + packed_sums(dot_nt(beside(dab0), layers_beside(su0)), picks[1])
+    for n in range(2):
+        pack[n] = sums[32 * n : 32 * n + 32]
 
     first = []
     for s in far_first:
         to, peer = in_group(s)
         copy = pltpu.make_async_remote_copy(
-            src_ref=pack.at[to], dst_ref=red_g.at[me_g],
+            src_ref=pack.at[lax.rem(to, 2)], dst_ref=red_g.at[me_g],
             send_sem=red_send.at[0, s], recv_sem=red_recv.at[0, s],
             device_id=peer, device_id_type=MESH,
         )
         copy.start()
         first.append(copy)
-    red_g[me_g] = pack[me_g]
+    red_g[me_g] = pack[core]
 
     pbuf[0] = jnp.zeros_like(pbuf[0])
     pbuf[1] = jnp.zeros_like(pbuf[1])
@@ -537,27 +542,21 @@
     for copy in third:
         copy.wait()
     tile_f[...] = sum_slots(red_z)
-    fourth = []
-    for s in far_first:
-        to, peer = in_group(s)
-        copy = pltpu.make_async_remote_copy(
-            src_ref=tile_f, dst_ref=final.at[me_g],
-            send_sem=red_send.at[3, s], recv_sem=red_recv.at[3, s],
-            device_id=peer, device_id_type=MESH,
-        )
-        copy.start()
-        fourth.append(copy)
-    final[me_g] = tile_f[...]
-    for copy in fourth:
-        copy.wait()
+    other = pltpu.make_async_remote_copy(
+        src_ref=tile_f, dst_ref=final.at[core],
+        send_sem=red_send.at[3, 0], recv_sem=red_recv.at[3, 0],
+        device_id=in_group(jnp.where(core > 0, 7, 1))[1], device_id_type=MESH,
+    )
+    other.start()
+    final[core] = tile_f[...]
+    other.wait()
 
     scale = 1.0 / 2048.0
     whole = final[...].reshape(CH, 128) * scale
     turned = whole.T
     for k in range(2):
-        out_w1[:, k, :] = turned[64 * k : 64 * k + 27, :]
-        out_w2[:, k, :] = turned[64 * k + 32 : 64 * k + 59, :]
-        out_b[k : k + 1, :] = turned[64 * k + 27 : 64 * k + 28, :]
+        out_p[:, k, 0:64] = turned[64 * k : 64 * k + 28, :]
+        out_p[0:27, k, 64:128] = turned[64 * k + 32 : 64 * k + 59, :]
 
 
 def sum_slots(store):
@@ -581,22 +580,22 @@
         stack, stack, stack, stack,
         vb(16 * CH, DEPTH), vb(12 * CH, DEPTH), vb(12 * CH, DEPTH), vb(8 * CH, DEPTH),
         vb(9 * GROWS, 16 * CH), vb(9 * GROWS, 12 * CH), vb(9 * GROWS, 8 * CH),
-        vm(2, 32, CH), vm(2, 32, CH),
+        vm(2, 32, CH), vm(2, 32, CH), vb(4, 256, 128),
         vm(16, 9 * GROWS, 128), vm(12, 9 * GROWS, 128),
         vb(5, 8 * CH, 256), vm(5, 8 * CH, 256), vb(5, 8 * CH, 256), vb(5, 8 * CH, 256), vb(4, 8 * CH, 256),
         vm(2, 8, 128), vm(2, 8, 128), vm(2, 2, 8, 128), vm(2, 8, 128), vm(2, 8, 128), vm(2, 2, 8, 128), vm(10, ROWS, 128),
-        vm(8, 8, 128), vm(8, 8, 128), vm(size_x // 4, 8, 128), vm(size_y // 2, 8, 128),
-        vm(8, 128), vm(8, 128), vm(8, 128), vm(8, 8, 128),
+        vm(2, 32, 128), vm(8, 32, 128), vm(size_x // 4, 32, 128), vm(size_y // 2, 32, 128),
+        vm(32, 128), vm(32, 128), vm(32, 128), vm(2, 32, 128),
         dma(6), dma(8), dma(8), dma(8), dma(8), dma(4, 8), dma(4, 8),
     ]
     spec = pl.BlockSpec(memory_space=pltpu.VMEM)
     far = pl.BlockSpec(memory_space=pltpu.HBM)
-    shapes = (vm(8, 8, 128), vm(27, 2, CH), vm(27, 2, CH), vm(2, CH))
-    grad, w1, w2, b = pl.pallas_call(
+    shapes = (vm(8, 8, 128), vm(28, 2, 128))
+    grad, sums = pl.pallas_call(
         functools.partial(kernel, size_x, size_y),
         out_shape=shapes,
         in_specs=[far] * 6,
-        out_specs=(spec,) * 4,
+        out_specs=(spec,) * 2,
         scratch_shapes=scratch,
         compiler_params=pltpu.CompilerParams(
             collective_id=0, has_side_effects=True, vmem_limit_bytes=60 * 1024 * 1024
@@ -605,6 +604,7 @@
         noisy, weights, jnp.transpose(filter_in, (2, 0, 1)), bias,
         jnp.transpose(filter_out, (1, 0, 2)), upstream,
     )
+    w1, w2, b = sums[:27, :, :64], sums[:27, :, 64:], sums[27, :, :64]
     return grad, jnp.transpose(w1, (1, 2, 0)), jnp.transpose(w2, (1, 0, 2)), b
 
 

time: 53.1 us -> 51.4 us (0.968)
  Pallas kernels: 49.9 us -> 48.7 us
    unnamed x4 -> x1, local copies, waits for them, and re-layouts: 2.4 us -> 0.62 us
    pallas_call x1, Pallas kernels: 49.9 us -> 48.7 us  [body(): pl.pallas_call(functools.partial(kernel, size_x, size_y), out_shape=shape...]
    transpose x0 -> x1, local copies, waits for them, and re-layouts: none -> 0.71 us  [body(): return (grad, jnp.transpose(w1, (1, 2, 0)), jnp.transpose(w2, (1, 0, 2)), b)]
    squeeze x0 -> x1, local copies, waits for them, and re-layouts: none -> 0.56 us  [body(): w1, w2, b = (sums[:27, :, :64], sums[:27, :, 64:], sums[27, :, :64])]
where the time goes in v4:
time: 51.4 us; the launch traced here: 51.2 us
  Pallas kernels  48.7 us (95%)
  local copies, waits for them, and re-layouts  1.89 us (4%)
  between operations  0.64 us (1%)
    pallas_call x1, Pallas kernels, body(): pl.pallas_call(functools.partial(kernel, size_x, size_y), out_shape=shape...  48.7 us

profile of v4, /device:TPU:1, one launch (start us, length us, event | category | flops | bytes accessed | tf_op | source)
XLA Modules:
  0.0 51.2 jit_solution(7606107613685805886)
XLA Ops:
  0.6 48.7 %shard_map.93 = (f32[8,8,128]{2,1,0:T(8,128)S(1)}, f32[28,2,128]{2,1,0:T(2,128)S(1)}) custom-call(f32[8,8,128]{2,1,0:T(8,128)} %noisy_at.1, f32[2,8,8,128]{3,2,1,0:T(8,128)} %weights_at.1, bf16[27,2,64]{2,1,0:T(2,128)(2,1)} %bitcast.8, f32[2,64]{1,0:T(2,128)} %bias_at.1, bf16[27,2,64]{2,1,0:T(2,128)(2,1)} %bitcast.9, f32[8,8,128]{2,1,0:T(8,128)} %upstream_at.1), custom_call_target="tpu_custom_call" | custom-call | tf_op jit(solution)/shard_map/pallas_call | solution.py:594
  49.3 0.6 %copy.11 = f32[8,8,128]{2,1,0:T(8,128)} copy(f32[8,8,128]{2,1,0:T(8,128)S(1)} %get-tuple-element.10) | data formatting | bytes 65536
  50.0 0.7 %slice_bitcast_fusion = (f32[2,27,64]{2,0,1:T(2,128)}, f32[2,64,27]{1,0,2:T(2,128)}) fusion(f32[28,2,128]{2,1,0:T(2,128)S(1)} %get-tuple-element.7), kind=kLoop, calls=%fused_computation | loop fusion | bytes 55296 | tf_op jit(solution)/shard_map/transpose | solution.py:608
  50.7 0.6 %slice_bitcast_fusion.2 = f32[2,64]{1,0:T(2,128)} fusion(f32[28,2,128]{2,1,0:T(2,128)S(1)} %get-tuple-element.7), kind=kLoop, calls=%fused_computation.2 | loop fusion | bytes 1024 | tf_op jit(solution)/shard_map/squeeze | solution.py:607

commit v5 on v4

--- a/solution.py
+++ b/solution.py
@@ -378,7 +378,7 @@
     def _(p):
         forward(p, False)
 
-    @pl.loop(2, 8, unroll=2)
+    @pl.loop(2, 8, unroll=3)
     def _(p):
         iterate(2 * p - 4)
         iterate(2 * p - 3)
@@ -419,7 +419,7 @@
     def _(p):
         middle(p, jnp.where(p > 0, 0, 4))
 
-    @pl.loop(2, 6, unroll=2)
+    @pl.loop(2, 6, unroll=4)
     def _(p):
         cotangent(2 * p - 4)
         cotangent(2 * p - 3)

time: 51.4 us -> 50.5 us (0.982)
  Pallas kernels: 48.7 us -> 47.8 us
    pallas_call x1, Pallas kernels: 48.7 us -> 47.8 us  [body(): pl.pallas_call(functools.partial(kernel, size_x, size_y), out_shape=shape...]
where the time goes in v5:
time: 50.5 us; the launch traced here: 50.4 us
  Pallas kernels  47.8 us (95%)
  local copies, waits for them, and re-layouts  1.89 us (4%)
  between operations  0.64 us (1%)
    pallas_call x1, Pallas kernels, body(): pl.pallas_call(functools.partial(kernel, size_x, size_y), out_shape=shape...  47.8 us

profile of v5, /device:TPU:1, one launch (start us, length us, event | category | flops | bytes accessed | tf_op | source)
XLA Modules:
  0.0 50.4 jit_solution(3167928075273511367)
XLA Ops:
  0.6 47.8 %shard_map.93 = (f32[8,8,128]{2,1,0:T(8,128)S(1)}, f32[28,2,128]{2,1,0:T(2,128)S(1)}) custom-call(f32[8,8,128]{2,1,0:T(8,128)} %noisy_at.1, f32[2,8,8,128]{3,2,1,0:T(8,128)} %weights_at.1, bf16[27,2,64]{2,1,0:T(2,128)(2,1)} %bitcast.8, f32[2,64]{1,0:T(2,128)} %bias_at.1, bf16[27,2,64]{2,1,0:T(2,128)(2,1)} %bitcast.9, f32[8,8,128]{2,1,0:T(8,128)} %upstream_at.1), custom_call_target="tpu_custom_call" | custom-call | tf_op jit(solution)/shard_map/pallas_call | solution.py:594
  48.5 0.6 %copy.11 = f32[8,8,128]{2,1,0:T(8,128)} copy(f32[8,8,128]{2,1,0:T(8,128)S(1)} %get-tuple-element.10) | data formatting | bytes 65536
  49.1 0.7 %slice_bitcast_fusion = (f32[2,27,64]{2,0,1:T(2,128)}, f32[2,64,27]{1,0,2:T(2,128)}) fusion(f32[28,2,128]{2,1,0:T(2,128)S(1)} %get-tuple-element.7), kind=kLoop, calls=%fused_computation | loop fusion | bytes 55296 | tf_op jit(solution)/shard_map/transpose | solution.py:608
  49.8 0.6 %slice_bitcast_fusion.2 = f32[2,64]{1,0:T(2,128)} fusion(f32[28,2,128]{2,1,0:T(2,128)S(1)} %get-tuple-element.7), kind=kLoop, calls=%fused_computation.2 | loop fusion | bytes 1024 | tf_op jit(solution)/shard_map/squeeze | solution.py:607
